TPU v7x, 256 devices: a whole 4x4x8 slice. The times are simulated.
256 devices in a mesh: gx: 64 (over y, x_hi, z), gz: 4 (over x_lo, core).
Axes of the slice: x: 4 (x_hi: 2, x_lo: 2; x = x_hi * 2 + x_lo), y: 4, z: 8, core: 2. Of those that a mesh axis runs over, the one named last changes fastest.
Arguments:
- solid_state: float32 [9, 20, 65536], P(None, None, ('gx', 'gz')), may hold values from -6 to 6
- jacobians: float32 [3, 9, 9, 65536], P(None, None, None, ('gx', 'gz')), may hold values from -2 to 2
- flux_solvers: float32 [4, 9, 9, 65536], P(None, None, None, ('gx', 'gz')), may hold values from -2 to 2
- stiffness: float32 [3, 20, 20], replicated, may hold values from -1.25 to 1.25
- trace_matrix: float32 [4, 10, 20], replicated, may hold values from -1.25 to 1.25
- lift_matrix: float32 [4, 20, 10], replicated, may hold values from -2 to 2
- neighbours: int32 [4, 65536], P(None, ('gx', 'gz')), may hold values from 0 to 1575, as said below
- send_faces: int32 [4, 32768], P(None, ('gx', 'gz')), may hold values from 0 to 1023, as said below
- surface_map: int32 [3, 5, 2048], P(None, None, ('gx', 'gz')), may hold values from 0 to 16383, as said below
- surface_normals: float32 [3, 5, 2048], P(None, None, ('gx', 'gz')), may hold values from -1 to 1
- air_state: float32 [4, 512, 64, 128], P(None, 'gx', 'gz'), may hold values from -6 to 6
- wind_field: float32 [3, 512, 64, 128], P(None, 'gx', 'gz'), may hold values from -0.3 to 0.3
- air_medium: float32 [2, 512, 64, 128], P(None, 'gx', 'gz'), may hold values from 0.05 to 0.25
Outputs:
- solid_next: float32 [9, 20, 65536], P(None, None, ('gx', 'gz'))
- air_next: float32 [4, 512, 64, 128], P(None, 'gx', 'gz')
Inputs may be any that keep to these rules, and one draw needn't show every extreme that they name: `neighbours`: entry [f, e] of a partition names what lies across face f of its tetrahedron e: below 1024 a face slot of the same partition (such slots name each other in pairs), from 1024 the slot 1024 + d * 128 + k of the k-th face shared in direction d, from 1536 the surface slot r * 8 + k. `send_faces`: the entries of a partition are distinct face slots; the face slot in [d, k] has neighbour entry 1024 + d * 128 + k. `surface_map`: row 0 holds distinct face slots, none of them in send_faces, whose neighbour entry is their surface slot; row 1 a cell index below 16384; row 2 is 1 for coupled slots and 0 otherwise. The coupled slots of one r are the lowest k; slots whose target strip lies outside 0 to 63 are uncoupled; the slots with r = 2 are all coupled.
All inputs are finite; a program needn't handle non-finite values.
Results may differ from a plain program's by a relative error of at most 0.0003.
Values sent between devices are 32-bit elements; how exact they have to be, the bound alone decides.
A program may use at most 128 MiB of HBM per device.

v0:
```python
import jax
import jax.numpy as jnp
from jax import lax
from jax.experimental import pallas as pl
from jax.experimental.pallas import tpu as pltpu
from jax.sharding import PartitionSpec as P

F32, BF16 = jnp.float32, jnp.bfloat16
MESH = pl.DeviceIdType.MESH

ORDERS = 4
TIME_STEP = 0.5
SUBSTEPS = 3
TAPS = (672.0, -168.0, 32.0, -3.0)
TAP_UNIT = 1.0 / 840.0

NQ, NB, NBP = 9, 20, 24
NJ, NJP = 10, 16
NT = 256
SLOTS = 4 * NT
RIM = 128
CAP, REACH = 8, 5
LEFT, RIGHT, BELOW, ABOVE = range(4)


def halves(x):
    high = x.astype(BF16)
    return high, (x - high.astype(F32)).astype(BF16)


def thirds(x):
    high = x.astype(BF16)
    rest = x - high.astype(F32)
    mid = rest.astype(BF16)
    return high, mid, (rest - mid.astype(F32)).astype(BF16)


def dot(a, b):
    return jnp.dot(a, b, preferred_element_type=F32)


def dot_nt(a, b):
    return lax.dot_general(a, b, (((1,), (1,)), ((), ())), preferred_element_type=F32)


def iota(shape, dim):
    return lax.broadcasted_iota(jnp.int32, shape, dim)


def stacked_left(padded, gap):
    high = padded.astype(BF16).astype(F32)
    low = padded - high
    return high + pltpu.roll(high, gap, 1) + pltpu.roll(low, 2 * gap, 1)


def lane_row(tile):
    total = tile[0:1]
    for r in range(1, REACH):
        total = total + pltpu.roll(tile, CAP * r, 1)[r : r + 1]
    return total


def kernel(strips, bands, *refs):
    (
        sol_h, jac_h, flx_h, stiff_ref, trace_ref, lift_ref, nbr_ref, surf_ref, normal_ref,
        air_h, wind_h, med_h,
        sol_out, air_out,
        sol, jac, flx, e0, e1, e2, e3, wind, med,
        ds, rot, integ, own, ohl, nmat, diff, vol, sout, uout,
        ksc, lsc, tsc, kp, kv, ts, ls, wy, smt, nmt,
        base, adv, a1, bt,
        ctile, stile, ptile, crecv, srecv, precv, tout, trecv, rl,
        local_sem, send_sem, recv_sem,
    ) = refs
    ext = (e0, e1, e2, e3)
    a = lax.axis_index("gx")
    b = lax.axis_index("gz")

    own_x, own_z = pl.ds(4, 8), pl.ds(8, 16)
    local = {}

    def fetch(name, src, dst):
        local[name] = pltpu.make_async_copy(src, dst, local_sem.at[len(local)])
        local[name].start()

    fetch("sol", sol_h, sol)
    fetch("jac", jac_h, jac)
    fetch("air", air_h, e0.at[:, own_x, own_z, :])
    fetch("wind", wind_h, wind)
    fetch("med", med_h, med)
    fetch("flx", flx_h, flx)

    can = {LEFT: a > 0, RIGHT: a < strips - 1, BELOW: b > 0, ABOVE: b < bands - 1}
    peer = {
        LEFT: (jnp.maximum(a - 1, 0), b),
        RIGHT: (jnp.minimum(a + 1, strips - 1), b),
        BELOW: (a, jnp.maximum(b - 1, 0)),
        ABOVE: (a, jnp.minimum(b + 1, bands - 1)),
    }
    mirror_of = {LEFT: RIGHT, RIGHT: LEFT, BELOW: ABOVE, ABOVE: BELOW}
    sem_count = [0]
    pending = []

    def next_sem():
        sem_count[0] += 1
        return sem_count[0] - 1

    def remote(src, dst, device, sem):
        return pltpu.make_async_remote_copy(
            src_ref=src, dst_ref=dst, send_sem=send_sem.at[sem], recv_sem=recv_sem.at[sem],
            device_id=device, device_id_type=MESH,
        )

    def exchange(make):
        sems = {d: next_sem() for d in range(4)}
        copies = {d: remote(*make(d), peer[d], sems[d]) for d in range(4)}
        for d in range(4):
            pl.when(can[d])(copies[d].start)
            pending.append((can[d], copies[d]))

        def arrive():
            for d in range(4):
                pl.when(can[d])(copies[mirror_of[d]].wait_recv)

        return arrive

    def surface(src, buffer, sign):
        waits = []
        for r in range(REACH):
            if r == 2:
                continue
            to = a + sign * (r - 2)
            source = a - sign * (r - 2)
            to_ok = (to >= 0) & (to < strips)
            from_ok = (source >= 0) & (source < strips)
            copy = remote(src, buffer.at[r], (jnp.clip(to, 0, strips - 1), b), next_sem())
            pl.when(to_ok)(copy.start)
            pending.append((to_ok, copy))
            waits.append((from_ok, copy))

        def arrive():
            for from_ok, copy in waits:
                pl.when(from_ok)(copy.wait_recv)

        return arrive

    x_send = {LEFT: pl.ds(4, 4), RIGHT: pl.ds(8, 4)}
    x_land = {LEFT: pl.ds(12, 4), RIGHT: pl.ds(0, 4)}
    z_send = {BELOW: pl.ds(8, 8), ABOVE: pl.ds(16, 8)}
    z_land = {BELOW: pl.ds(24, 8), ABOVE: pl.ds(0, 8)}

    def halo(buffer, fields):
        def make(d):
            if d in (LEFT, RIGHT):
                return buffer.at[fields, x_send[d], own_z, :], buffer.at[fields, x_land[d], own_z, :]
            return buffer.at[fields, own_x, z_send[d], :], buffer.at[fields, own_x, z_land[d], :]

        return make

    speeds_of, pressure_of = pl.ds(1, 3), pl.ds(0, 1)

    def halo_first(d):
        x_from = {LEFT: pl.ds(0, 4), RIGHT: pl.ds(4, 4)}
        z_from = {BELOW: pl.ds(0, 8), ABOVE: pl.ds(8, 8)}
        if d in (LEFT, RIGHT):
            return air_h.at[speeds_of, x_from[d]], e0.at[speeds_of, x_land[d], own_z, :]
        return air_h.at[speeds_of, :, z_from[d], :], e0.at[speeds_of, own_x, z_land[d], :]

    for d, where in ((LEFT, pl.ds(0, 4)), (RIGHT, pl.ds(12, 4))):
        @pl.when(jnp.logical_not(can[d]))
        def _(where=where):
            for buffer in (e0, e1, e2):
                buffer[:, where, own_z, :] = jnp.zeros((4, 4, 16, 128), F32)
            e3[pressure_of, where, own_z, :] = jnp.zeros((1, 4, 16, 128), F32)
    for d, where in ((BELOW, pl.ds(0, 8)), (ABOVE, pl.ds(24, 8))):
        @pl.when(jnp.logical_not(can[d]))
        def _(where=where):
            for buffer in (e0, e1, e2):
                buffer[:, own_x, where, :] = jnp.zeros((4, 8, 8, 128), F32)
            e3[pressure_of, own_x, where, :] = jnp.zeros((1, 8, 8, 128), F32)
    crecv[...] = jnp.zeros_like(crecv)
    srecv[...] = jnp.zeros_like(srecv)
    precv[...] = jnp.zeros_like(precv)
    trecv[...] = jnp.zeros_like(trecv)

    barrier = pltpu.get_barrier_semaphore()
    for off in (-2, -1, 1, 2):
        pl.semaphore_signal(
            barrier, inc=1, device_id=(lax.rem(a + off + strips, strips), b), device_id_type=MESH
        )
    for off in (-1, 1):
        pl.semaphore_signal(
            barrier, inc=1, device_id=(a, lax.rem(b + off + bands, bands)), device_id_type=MESH
        )

    smt[...] = jnp.zeros_like(smt)
    nmt[...] = jnp.zeros_like(nmt)
    for i in range(3):
        smt[i, 0:REACH, 0:CAP] = surf_ref[i].astype(F32)
        nmt[i, 0:REACH, 0:CAP] = normal_ref[i]
    own_cells = lane_row(smt[1])
    coupled = lane_row(smt[2])
    normals = [lane_row(nmt[c]) for c in range(3)]
    ctile[...] = jnp.broadcast_to(own_cells, (8, 128))

    ksc[...] = jnp.zeros_like(ksc)
    tsc[...] = jnp.zeros_like(tsc)
    lsc[...] = jnp.zeros_like(lsc)
    for d in range(3):
        ksc[d * NBP : d * NBP + NB, 0:NB] = stiff_ref[d]
    for f in range(4):
        rows = trace_ref[f]
        tsc[f * NJP : f * NJP + NJ, 0:NB] = rows
        tsc[f * NJP + NJ : f * NJP + NJ + 1, 0:NB] = jnp.sum(rows, axis=0, keepdims=True) * (1.0 / NJ)
        lsc[f, 0:NB, 0:NJ] = lift_ref[f]
    stiff = ksc[...]
    kp[...] = (-stacked_left(stiff[0:80], 32)).astype(BF16)
    flipped = jnp.transpose(stiff)[0:NBP]
    lanes = iota((NBP, 128), 1)
    turned = [jnp.where(lanes < NBP, flipped if d == 0 else pltpu.roll(flipped, 128 - d * NBP, 1), 0.0) for d in range(3)]
    turned.append(jnp.zeros((8, 128), F32))
    kv[...] = stacked_left(jnp.concatenate(turned, axis=0), 32).astype(BF16)
    ts[...] = stacked_left(tsc[...], 32).astype(BF16)
    lift = lsc[0]
    for f in range(1, 4):
        lift = lift + pltpu.roll(lsc[f], f * NJP, 1)
    lift_high = lift.astype(BF16).astype(F32)
    ls[:, 0:128] = (lift_high + pltpu.roll(lift_high, 64, 1)).astype(BF16)
    ls[:, 128:256] = (lift - lift_high).astype(BF16)
    shift = lax.rem(iota((256, 128), 0), 128) - iota((256, 128), 1)
    taps = jnp.zeros((256, 128), F32)
    for m, tap in enumerate(TAPS, 1):
        taps = jnp.where(shift == m, tap, jnp.where(shift == -m, -tap, taps))
    wy[...] = taps.astype(BF16)
    ds[:, 96:128, :] = jnp.zeros((NQ, 32, NT), BF16)

    def onehot_rows(start, count):
        names = iota((count, NT), 0) + start
        return [jnp.where(names == nbr_ref[f : f + 1, :], 1.0, 0.0).astype(BF16) for f in range(4)]

    for f, block in enumerate(onehot_rows(1536, 128)):
        nmat[1536:1664, f * NT : (f + 1) * NT] = block

    pl.semaphore_wait(barrier, 6)
    cells_arrive = surface(ctile, crecv, 1)
    first_arrive = exchange(halo_first)

    def put_stack(q, x):
        high, low = halves(jnp.concatenate([x, jnp.zeros((8, NT), F32)], axis=0))
        ds[q, 0:32, :] = high
        ds[q, 32:64, :] = low
        ds[q, 64:96, :] = high

    def rotate(left):
        for q in range(NQ):
            rot[q] = dot(left[...], ds[q])

    def contract(p0):
        total = None
        for q in range(NQ):
            for d in range(3):
                term = jac[d, pl.ds(p0, 3), pl.ds(q, 1), :] * rot[q, d * NBP : (d + 1) * NBP, :][None]
                total = term if total is None else total + term
        return total

    local["sol"].wait()
    integ[...] = jnp.zeros_like(integ)
    for q in range(NQ):
        integ[q, 0:NB, :] = TIME_STEP * sol[q]
    for q in range(NQ):
        put_stack(q, integ[q] * (1.0 / TIME_STEP))
    local["jac"].wait()
    weight = TIME_STEP
    for degree in range(1, ORDERS):
        weight = weight * TIME_STEP / (degree + 1)
        rotate(kp)

        def step(i, carry, weight=weight, last=degree == ORDERS - 1):
            now = contract(3 * i)
            for k in range(3):
                total = integ[3 * i + k] + weight * now[k]
                integ[3 * i + k] = total
                put_stack(3 * i + k, total if last else now[k])
            return carry

        lax.fori_loop(0, 3, step, 0)

    for q in reversed(range(NQ)):
        traces = dot(ts[...], ds[q])
        own[q] = traces
        high, low = halves(traces)
        for f in range(4):
            rows, cols = slice(f * NJP, (f + 1) * NJP), slice(f * NT, (f + 1) * NT)
            ohl[q * NJP : (q + 1) * NJP, cols] = high[rows]
            ohl[(NQ + q) * NJP : (NQ + q + 1) * NJP, cols] = low[rows]
    surf_names = nmat[1536:1664, :]
    at_faces = dot_nt(ohl[96:144, :], surf_names) + dot_nt(ohl[240:288, :], surf_names)
    speed = jnp.zeros((1, 128), F32)
    for c in range(3):
        speed = speed + normals[c] * at_faces[c * NJP + NJ : c * NJP + NJ + 1, :]
    own_speed = coupled * speed
    stile[...] = jnp.broadcast_to(own_speed, (8, 128))
    speeds_arrive = surface(stile, srecv, 1)

    slot_row = iota((1, 128), 1) // CAP

    def combine(mine, buffer, sign):
        total = jnp.where(slot_row == 2, mine, 0.0)
        for r in range(REACH):
            if r != 2:
                source = a - sign * (r - 2)
                ok = (source >= 0) & (source < strips)
                total = jnp.where(slot_row == jnp.where(ok, r, -1), buffer[r, 0:1, :], total)
        return total

    cells_arrive()
    cells = combine(own_cells, crecv, 1).astype(jnp.int32)
    cell_rows = lax.shift_right_logical(cells, 7)
    cell_lanes = lax.bitwise_and(cells, 127)
    a1[...] = jnp.where(iota((128, 128), 0) == cell_rows, 1.0, 0.0)
    bt[...] = jnp.where(iota((128, 128), 0) == cell_lanes, 1.0, 0.0)
    local["air"].wait()
    pressure = e0[0, own_x, own_z, :].reshape(128, 128)
    at_lane = bt[...].astype(BF16)
    picked = dot(jnp.concatenate(thirds(pressure), axis=0), at_lane)
    picked = picked[0:128] + picked[128:256] + picked[256:384]
    looked = jnp.sum(picked * a1[...], axis=0, keepdims=True)
    ptile[...] = jnp.broadcast_to(looked, (8, 128))
    replies_arrive = surface(ptile, precv, -1)

    def along_x(ref, f):
        total = None
        for m, tap in enumerate(TAPS, 1):
            term = tap * (ref[f, 4 + m : 12 + m, 8:24, :] - ref[f, 4 - m : 12 - m, 8:24, :])
            total = term if total is None else total + term
        return total

    def along_z(ref, f):
        total = None
        for m, tap in enumerate(TAPS, 1):
            term = tap * (ref[f, 4:12, 8 + m : 24 + m, :] - ref[f, 4:12, 8 - m : 24 - m, :])
            total = term if total is None else total + term
        return total

    def along_y(ref, f):
        x = ref[f, 4:12, 8:24, :].reshape(128, 128)
        return dot(jnp.concatenate(halves(x), axis=1), wy[...]).reshape(8, 16, 128)

    def store_divergence(ref, into):
        into[...] = ref[0, 4:12, 8:24, :] - med[0] * (along_x(ref, 1) + along_z(ref, 2) + along_y(ref, 3))

    def advected(ref, f):
        return wind[0] * along_x(ref, f) + wind[1] * along_z(ref, f) + wind[2] * along_y(ref, f)

    local["wind"].wait()
    local["med"].wait()
    wind[...] = wind[...] * TAP_UNIT
    med[...] = med[...] * TAP_UNIT

    def names_block(i, carry):
        start = pl.multiple_of(64 * i, 64)
        for f, block in enumerate(onehot_rows(start, 64)):
            nmat[pl.ds(start, 64), f * NT : (f + 1) * NT] = block
        return carry

    first_arrive()
    store_divergence(e0, base)

    speeds_arrive()
    arrived = combine(own_speed, srecv, 1)
    at_row = jnp.concatenate(thirds(a1[...] * arrived), axis=1)
    injected = dot_nt(at_row, jnp.concatenate([at_lane] * 3, axis=1)).reshape(8, 16, 128)
    e0[0, own_x, own_z, :] = e0[0, own_x, own_z, :] + injected
    base[...] = base[...] + injected
    pressure_arrive = exchange(halo(e0, pressure_of))

    lax.fori_loop(0, 24, names_block, 0)
    given = dot_nt(ohl[...], nmat[1024:1664, :])
    given = given[0:144] + given[144:288]
    for d in range(4):
        for q in range(NQ):
            tout[d, q * NJ : (q + 1) * NJ, :] = given[q * NJP : q * NJP + NJ, d * RIM : (d + 1) * RIM]
    traces_arrive = exchange(lambda d: (tout.at[d], trecv.at[mirror_of[d]]))
    own_at = given[:, 512:640]

    def shadow_first():
        for f in range(4):
            cols = slice(f * NT, (f + 1) * NT)
            gathered = dot(ohl[...], nmat[0:SLOTS, cols])
            gathered = gathered[0:144] + gathered[144:288]
            for q in range(NQ):
                rows = slice(f * NJP, (f + 1) * NJP)
                diff[q, rows, :] = gathered[q * NJP : (q + 1) * NJP] - own[q, rows, :]

    def shadow_second():
        rotate(kv)

        def step(i, carry):
            vol[pl.ds(3 * i, 3)] = contract(3 * i)
            return carry

        lax.fori_loop(0, 3, step, 0)

    def shadow_third():
        replies_arrive()
        traces_arrive()
        replies = coupled * combine(looked, precv, -1)
        row_q = iota((NQ * NJP, 128), 0) // NJP
        mirrored = jnp.where(row_q < 3, -2.0 * replies - own_at, own_at)
        for half, values in enumerate(halves(mirrored)):
            rl[half * 144 : half * 144 + 144, 512:640] = values
        for d in range(4):
            for q in range(NQ):
                x = jnp.concatenate([trecv[d, q * NJ : (q + 1) * NJ, :], jnp.zeros((NJP - NJ, RIM), F32)], axis=0)
                for half, values in enumerate(halves(x)):
                    start = half * 144 + q * NJP
                    rl[start : start + NJP, d * RIM : (d + 1) * RIM] = values
        for f in range(4):
            cols = slice(f * NT, (f + 1) * NT)
            gathered = dot(rl[...], nmat[SLOTS:1664, cols])
            gathered = gathered[0:144] + gathered[144:288]
            for q in range(NQ):
                rows = slice(f * NJP, (f + 1) * NJP)
                diff[q, rows, :] = diff[q, rows, :] + gathered[q * NJP : (q + 1) * NJP]

    def shadow_fourth():
        local["flx"].wait()

        def step(i, carry):
            faces = []
            for f in range(4):
                total = None
                for q in range(NQ):
                    term = flx[f, pl.ds(3 * i, 3), pl.ds(q, 1), :] * diff[q, f * NJP : (f + 1) * NJP, :][None]
                    total = term if total is None else total + term
                faces.append(total)
            fluxed = jnp.concatenate(faces, axis=1)
            for k in range(3):
                high, low = halves(fluxed[k])
                lifted = dot(ls[:, 0:192], jnp.concatenate([high, low, high], axis=0))
                p = 3 * i + k
                sout[p] = sol[p] + (vol[p] + lifted[0:NBP])[0:NB]
            return carry

        lax.fori_loop(0, 3, step, 0)

    shadows = {1: shadow_first, 2: shadow_second, 3: shadow_third, 4: shadow_fourth}
    turn = 0
    for substep in range(SUBSTEPS):
        here, there = ext[substep], ext[substep + 1]
        final = substep == SUBSTEPS - 1
        if substep == 0:
            pressure_arrive()
            base[...] = base[...] - advected(here, 0)
        else:
            velocity_arrive()
            base[...] = base[...] - med[0] * (along_x(here, 1) + along_z(here, 2) + along_y(here, 3))
        there[0, own_x, own_z, :] = base[...]
        pressure_arrive = exchange(halo(there, pressure_of))
        for f in range(3):
            adv[f] = here[1 + f, own_x, own_z, :] - advected(here, 1 + f)
        turn += 1
        if turn in shadows:
            shadows[turn]()
        pressure_arrive()
        slopes = (along_x(there, 0), along_z(there, 0), along_y(there, 0))
        if final:
            for f in range(3):
                uout[1 + f] = adv[f] - med[1] * slopes[f]
            uout[0] = there[0, own_x, own_z, :]
        else:
            for f in range(3):
                there[1 + f, own_x, own_z, :] = adv[f] - med[1] * slopes[f]
            velocity_arrive = exchange(halo(there, speeds_of))
            base[...] = there[0, own_x, own_z, :] - (
                wind[0] * slopes[0] + wind[1] * slopes[1] + wind[2] * slopes[2]
            )
            turn += 1
            if turn in shadows:
                shadows[turn]()

    fetch("sol_out", sout, sol_out)
    fetch("air_out", uout, air_out)
    local["sol_out"].wait()
    local["air_out"].wait()
    for ok, copy in pending:
        pl.when(ok)(copy.wait_send)


def vmem(*shape, dtype=F32):
    return pltpu.VMEM(shape, dtype)


def solution(mesh):
    strips, bands = mesh.shape["gx"], mesh.shape["gz"]

    def shards(
        solid_state, jacobians, flux_solvers, stiffness, trace_matrix, lift_matrix,
        neighbours, send_faces, surface_map, surface_normals, air_state, wind_field, air_medium,
    ):
        def body(*refs):
            kernel(strips, bands, *refs)

        hbm = pl.BlockSpec(memory_space=pl.ANY)
        near = pl.BlockSpec(memory_space=pltpu.VMEM)
        return pl.pallas_call(
            body,
            out_shape=(
                jax.ShapeDtypeStruct(solid_state.shape, F32),
                jax.ShapeDtypeStruct(air_state.shape, F32),
            ),
            in_specs=[hbm, hbm, hbm, near, near, near, near, near, near, hbm, hbm, hbm],
            out_specs=(hbm, hbm),
            scratch_shapes=[
                vmem(NQ, NB, NT), vmem(3, NQ, NQ, NT), vmem(4, NQ, NQ, NT),
                vmem(4, 16, 32, 128), vmem(4, 16, 32, 128), vmem(4, 16, 32, 128), vmem(4, 16, 32, 128),
                vmem(3, 8, 16, 128), vmem(2, 8, 16, 128),
                vmem(NQ, 128, NT, dtype=BF16), vmem(NQ, 80, NT), vmem(NQ, NBP, NT), vmem(NQ, 64, NT),
                vmem(288, SLOTS, dtype=BF16), vmem(1664, SLOTS, dtype=BF16), vmem(NQ, 64, NT),
                vmem(NQ, NBP, NT), vmem(NQ, NB, NT), vmem(4, 8, 16, 128),
                vmem(128, 128), vmem(4, 32, 128), vmem(64, 128),
                vmem(80, 128, dtype=BF16), vmem(80, 128, dtype=BF16), vmem(64, 128, dtype=BF16),
                vmem(32, 256, dtype=BF16), vmem(256, 128, dtype=BF16),
                vmem(3, 8, 128), vmem(3, 8, 128),
                vmem(8, 16, 128), vmem(3, 8, 16, 128), vmem(128, 128), vmem(128, 128),
                vmem(8, 128), vmem(8, 128), vmem(8, 128),
                vmem(REACH, 8, 128), vmem(REACH, 8, 128), vmem(REACH, 8, 128),
                vmem(4, 96, RIM), vmem(4, 96, RIM), vmem(288, 640, dtype=BF16),
                pltpu.SemaphoreType.DMA((8,)),
                pltpu.SemaphoreType.DMA((48,)),
                pltpu.SemaphoreType.DMA((48,)),
            ],
            compiler_params=pltpu.CompilerParams(
                collective_id=0, has_side_effects=True, vmem_limit_bytes=56 * 1024 * 1024
            ),
            name="coupled_step",
        )(
            solid_state, jacobians, flux_solvers, stiffness, trace_matrix, lift_matrix,
            neighbours, surface_map, surface_normals, air_state, wind_field, air_medium,
        )

    in_specs = (
        P(None, None, ("gx", "gz")),
        P(None, None, None, ("gx", "gz")),
        P(None, None, None, ("gx", "gz")),
        P(),
        P(),
        P(),
        P(None, ("gx", "gz")),
        P(None, ("gx", "gz")),
        P(None, None, ("gx", "gz")),
        P(None, None, ("gx", "gz")),
        P(None, "gx", "gz", None),
        P(None, "gx", "gz", None),
        P(None, "gx", "gz", None),
    )
    out_specs = (P(None, None, ("gx", "gz")), P(None, "gx", "gz", None))
    return jax.shard_map(shards, mesh=mesh, in_specs=in_specs, out_specs=out_specs, check_vma=False)
```

profile of v0, /device:TPU:25, one launch (start us, length us, event | category | flops | bytes accessed | tf_op | source)
XLA Modules:
  0.0 61.2 jit_solution(2069196245031222911)
XLA Ops:
  0.6 0.0 copy-start.4
  0.6 0.0 copy-start.2
  0.7 1.3 %copy.18.refs_7_ = s32[3,5,8]{2,1,0:T(8,128)} copy(s32[3,5,8]{2,0,1:T(4,128)} %param.20) | data formatting | bytes 960 | tf_op args[8]
  2.0 0.0 copy-done.4
  2.0 0.6 copy.19.refs_8_
  2.6 0.0 copy-done.2
  2.6 0.0 copy-start.3
  2.6 0.6 %copy.16.refs_4_ = f32[4,10,20]{2,1,0:T(8,128)} copy(f32[4,10,20]{2,0,1:T(4,128)S(1)} %copy-done.2) | data formatting | bytes 6400 | tf_op args[4]
  3.2 0.1 copy-done.3
  3.3 0.7 %copy.17.refs_5_ = f32[4,20,10]{2,1,0:T(8,128)} copy(f32[4,20,10]{1,0,2:T(4,128)S(1)} %copy-done.3) | data formatting | bytes 6400 | tf_op args[5]
  4.0 0.0 copy-start
  4.0 1.8 %copy.14.refs_1_ = f32[3,9,9,256]{3,2,1,0:T(8,128)} copy(f32[3,9,9,256]{3,0,2,1:T(4,128)} %param.14) | data formatting | bytes 497664 | tf_op args[1]
  5.9 0.0 copy-done
  5.9 0.9 %copy.15.refs_2_ = f32[4,9,9,256]{3,2,1,0:T(8,128)} copy(f32[4,9,9,256]{3,0,2,1:T(4,128)S(1)} %copy-done) | data formatting | bytes 663552 | tf_op args[2]
  6.8 52.0 %coupled_step.1 = (f32[9,20,256]{2,1,0:T(8,128)}, f32[4,8,16,128]{3,2,1,0:T(8,128)}) custom-call(f32[9,20,256]{2,1,0:T(8,128)} %refs_0_.1, f32[3,9,9,256]{3,2,1,0:T(8,128)} %copy.14.refs_1_, f32[4,9,9,256]{3,2,1,0:T(8,128)} %copy.15.refs_2_, f32[3,20,20]{2,1,0:T(8,128)} %refs_3_.1, f32[4,10,20]{2,1,0:T(8,128)} %copy.16.refs_4_, f32[4,20,10]{2,1,0:T(8,128)} %copy.17.refs_5_, ...), custom_call_target="tpu_custom_call" | custom-call | tf_op jit(solution)/shard_map/coupled_step/pallas_call | solution.py:506
  58.8 0.0 copy-start.1
  58.8 1.7 %copy.22 = f32[9,20,256]{2,1,0:T(8,128)} copy(f32[9,20,256]{2,1,0:T(8,128)} %get-tuple-element.4) | data formatting | bytes 368640
  60.5 0.0 copy-done.1
  60.5 0.7 %copy.23 = f32[4,8,16,128]{3,2,1,0:T(8,128)} copy(f32[4,8,16,128]{3,2,1,0:T(8,128)S(1)} %copy-done.1) | data formatting | bytes 524288
Async XLA Ops:
  0.6 1.3 %copy-start.4 = (f32[3,5,8]{2,0,1:T(4,128)S(1)}, f32[3,5,8]{2,0,1:T(4,128)}, u32[]{:S(2)}) copy-start(f32[3,5,8]{2,0,1:T(4,128)} %param.21) | copy-start | bytes 1444
  0.6 1.9 %copy-start.2 = (f32[4,10,20]{2,0,1:T(4,128)S(1)}, f32[4,10,20]{2,0,1:T(4,128)}, u32[]{:S(2)}) copy-start(f32[4,10,20]{2,0,1:T(4,128)} %param.17) | copy-start | bytes 9604
  2.6 0.7 %copy-start.3 = (f32[4,20,10]{1,0,2:T(4,128)S(1)}, f32[4,20,10]{1,0,2:T(4,128)}, u32[]{:S(2)}) copy-start(f32[4,20,10]{1,0,2:T(4,128)} %param.18) | copy-start | bytes 9604
  4.0 1.9 %copy-start = (f32[4,9,9,256]{3,0,2,1:T(4,128)S(1)}, f32[4,9,9,256]{3,0,2,1:T(4,128)}, u32[]{:S(2)}) copy-start(f32[4,9,9,256]{3,0,2,1:T(4,128)} %param.15) | copy-start | bytes 995332
  58.8 1.7 %copy-start.1 = (f32[4,8,16,128]{3,2,1,0:T(8,128)S(1)}, f32[4,8,16,128]{3,2,1,0:T(8,128)}, u32[]{:S(2)}) copy-start(f32[4,8,16,128]{3,2,1,0:T(8,128)} %get-tuple-element.5) | copy-start | bytes 786436
where the time goes:
time: 61.5 us; the launch traced here: 61.2 us
  Pallas kernels  52 us (85%)
  local copies, waits for them, and re-layouts  8.52 us (14%)
  between operations  0.67 us (1%)
    pallas_call x1, Pallas kernels, shards(): pl.pallas_call(body, out_shape=(jax.ShapeDtypeStruct(solid_state.shape, F...  52 us
    unnamed x18, local copies, waits for them, and re-layouts  8.52 us

commit v1 on v0

v1 whole, which is shorter than its diff:
```python
import jax
import jax.numpy as jnp
from jax import lax
from jax.experimental import pallas as pl
from jax.experimental.pallas import tpu as pltpu
from jax.sharding import PartitionSpec as P

F32, BF16 = jnp.float32, jnp.bfloat16
MESH = pl.DeviceIdType.MESH

ORDERS = 4
TIME_STEP = 0.5
SUBSTEPS = 3
TAPS = (672.0, -168.0, 32.0, -3.0)
TAP_UNIT = 1.0 / 840.0

NQ, NB, NBP = 9, 20, 24
NJ, NJP = 10, 16
NT = 256
SLOTS = 4 * NT
RIM = 128
CAP, REACH = 8, 5
LEFT, RIGHT, BELOW, ABOVE = range(4)


def halves(x):
    high = x.astype(BF16)
    return high, (x - high.astype(F32)).astype(BF16)


def thirds(x):
    high = x.astype(BF16)
    rest = x - high.astype(F32)
    mid = rest.astype(BF16)
    return high, mid, (rest - mid.astype(F32)).astype(BF16)


def dot(a, b):
    return jnp.dot(a, b, preferred_element_type=F32)


def dot_nt(a, b):
    return lax.dot_general(a, b, (((1,), (1,)), ((), ())), preferred_element_type=F32)


def iota(shape, dim):
    return lax.broadcasted_iota(jnp.int32, shape, dim)


def stacked_left(padded, gap):
    high = padded.astype(BF16).astype(F32)
    low = padded - high
    return high + pltpu.roll(high, gap, 1) + pltpu.roll(low, 2 * gap, 1)


def lane_row(tile):
    total = tile[0:1]
    for r in range(1, REACH):
        total = total + pltpu.roll(tile, CAP * r, 1)[r : r + 1]
    return total


def kernel(strips, bands, *refs):
    (
        sol_h, jac_h, flx_h, stiff_h, trace_h, lift_h, nbr_h, surf_h, normal_h,
        air_h, wind_h, med_h,
        sol_out, air_out,
        stiff_ref, trace_ref, lift_ref, nbr_ref, surf_ref, normal_ref,
        sol, jac, flx, e0, e1, e2, coef, pe, lift_of,
        ds, rot, integ, own, ohl, nmat, diff, vol, sout, uout,
        ksc, lsc, tsc, kp, kv, ts, ls, wy, smt, nmt,
        base, adv, start_pressure, gained, bt,
        stile, ptile, srecv, precv, tout, trecv, rl,
        local_sem, send_sem, recv_sem,
    ) = refs
    ext = (e0, e1, e2)
    a = lax.axis_index("gx")
    b = lax.axis_index("gz")

    own_x, own_z = pl.ds(8, 8), pl.ds(16, 16)
    coef_x_own, coef_z_own = pl.ds(4, 8), pl.ds(8, 16)
    local = {}

    def fetch(name, src, dst):
        local[name] = pltpu.make_async_copy(src, dst, local_sem.at[len(local)])
        local[name].start()

    fetch("stiff", stiff_h, stiff_ref)
    fetch("sol", sol_h, sol)
    fetch("jac", jac_h, jac)
    fetch("trace", trace_h, trace_ref)
    fetch("nbr", nbr_h, nbr_ref)
    fetch("surf", surf_h, surf_ref)
    fetch("normal", normal_h, normal_ref)
    fetch("air", air_h, e0.at[:, own_x, own_z, :])
    fetch("wind", wind_h, coef.at[pl.ds(0, 3), coef_x_own, coef_z_own])
    fetch("bulk", med_h.at[0], coef.at[3, coef_x_own, coef_z_own])
    fetch("lift", med_h.at[1], lift_of)
    fetch("flx", flx_h, flx)
    fetch("lifting", lift_h, lift_ref)

    can = {LEFT: a > 0, RIGHT: a < strips - 1, BELOW: b > 0, ABOVE: b < bands - 1}
    peer = {
        LEFT: (jnp.maximum(a - 1, 0), b),
        RIGHT: (jnp.minimum(a + 1, strips - 1), b),
        BELOW: (a, jnp.maximum(b - 1, 0)),
        ABOVE: (a, jnp.minimum(b + 1, bands - 1)),
    }
    mirror_of = {LEFT: RIGHT, RIGHT: LEFT, BELOW: ABOVE, ABOVE: BELOW}
    sem_count = [0]
    pending = []

    def remote(src, dst, device, sem):
        return pltpu.make_async_remote_copy(
            src_ref=src, dst_ref=dst, send_sem=send_sem.at[sem], recv_sem=recv_sem.at[sem],
            device_id=device, device_id_type=MESH,
        )

    def exchange(parts):
        copies = []
        for d, src, dst in parts:
            ok, device = side(d)
            copy = remote(src, dst, device, sem_count[0])
            sem_count[0] += 1
            pl.when(ok)(copy.start)
            pending.append((ok, copy))
            copies.append((d, copy))

        def arrive():
            for d, copy in copies:
                pl.when(side(opposite(d))[0])(copy.wait_recv)

        return arrive

    def opposite(d):
        return tuple(mirror_of[k] for k in d) if isinstance(d, tuple) else mirror_of[d]

    def side(d):
        if isinstance(d, tuple):
            return can[d[0]] & can[d[1]], (peer[d[0]][0], peer[d[1]][1])
        return can[d], peer[d]

    def surface(src, place, sign, reach):
        waits = []
        for off in (3, -3, 2, -2, 1, -1):
            if abs(off) > reach:
                continue
            to = a + sign * off
            source = a - sign * off
            to_ok = (to >= 0) & (to < strips)
            from_ok = (source >= 0) & (source < strips)
            copy = remote(src, place(off), (jnp.clip(to, 0, strips - 1), b), sem_count[0])
            sem_count[0] += 1
            pl.when(to_ok)(copy.start)
            pending.append((to_ok, copy))
            waits.append((from_ok, copy))

        def arrive():
            for from_ok, copy in waits:
                pl.when(from_ok)(copy.wait_recv)

        return arrive

    diagonals = ((LEFT, BELOW), (LEFT, ABOVE), (RIGHT, BELOW), (RIGHT, ABOVE))
    x_near = {LEFT: pl.ds(8, 4), RIGHT: pl.ds(12, 4)}
    x_far = {LEFT: pl.ds(12, 4), RIGHT: pl.ds(8, 4)}
    near_land = {LEFT: pl.ds(16, 4), RIGHT: pl.ds(4, 4)}
    far_land = {LEFT: pl.ds(20, 4), RIGHT: pl.ds(0, 4)}
    all_land = {LEFT: pl.ds(16, 8), RIGHT: pl.ds(0, 8)}
    z_near = {BELOW: pl.ds(16, 8), ABOVE: pl.ds(24, 8)}
    z_land = {BELOW: pl.ds(32, 8), ABOVE: pl.ds(8, 8)}
    raw_x = {LEFT: pl.ds(0, 4), RIGHT: pl.ds(4, 4)}
    raw_z = {BELOW: pl.ds(0, 8), ABOVE: pl.ds(8, 8)}
    coef_x = {LEFT: pl.ds(12, 4), RIGHT: pl.ds(0, 4)}
    coef_z = {BELOW: pl.ds(24, 8), ABOVE: pl.ds(0, 8)}
    with_arms = pl.ds(4, 16)

    def send_speeds(buffer, raw=None):
        parts = []
        for d in (LEFT, RIGHT):
            if raw is None:
                parts.append((d, buffer.at[1, own_x, own_z], buffer.at[1, all_land[d], own_z]))
                parts.append((d, buffer.at[pl.ds(2, 2), x_near[d], own_z], buffer.at[pl.ds(2, 2), near_land[d], own_z]))
            else:
                parts.append((d, raw.at[1], buffer.at[1, all_land[d], own_z]))
                parts.append((d, raw.at[pl.ds(2, 2), raw_x[d]], buffer.at[pl.ds(2, 2), near_land[d], own_z]))
        for d in diagonals:
            src = buffer.at[pl.ds(1, 2), x_near[d[0]], z_near[d[1]]]
            if raw is not None:
                src = raw.at[pl.ds(1, 2), raw_x[d[0]], raw_z[d[1]]]
            parts.append((d, src, buffer.at[pl.ds(1, 2), near_land[d[0]], z_land[d[1]]]))
        for d in (BELOW, ABOVE):
            src = buffer.at[pl.ds(1, 3), own_x, z_near[d]]
            if raw is not None:
                src = raw.at[pl.ds(1, 3), :, raw_z[d]]
            parts.append((d, src, buffer.at[pl.ds(1, 3), own_x, z_land[d]]))
        return exchange(parts)

    def send_pressure_z(buffer):
        return [(d, buffer.at[0, with_arms, z_near[d]], buffer.at[0, with_arms, z_land[d]]) for d in (BELOW, ABOVE)]

    def send_pressure(buffer):
        parts = [(d, buffer.at[0, x_far[d], own_z], buffer.at[0, far_land[d], own_z]) for d in (LEFT, RIGHT)]
        return exchange(parts + send_pressure_z(buffer))

    def send_first():
        first = exchange([(d, air_h.at[0], e0.at[0, all_land[d], own_z]) for d in (LEFT, RIGHT)])
        second = send_speeds(e0, air_h)
        parts = []
        for d in (LEFT, RIGHT):
            parts.append((d, wind_h.at[:, raw_x[d]], coef.at[pl.ds(0, 3), coef_x[d], coef_z_own]))
            parts.append((d, med_h.at[0, raw_x[d]], coef.at[3, coef_x[d], coef_z_own]))
        for d in (BELOW, ABOVE):
            parts.append((d, wind_h.at[:, :, raw_z[d]], coef.at[pl.ds(0, 3), coef_x_own, coef_z[d]]))
            parts.append((d, med_h.at[0, :, raw_z[d]], coef.at[3, coef_x_own, coef_z[d]]))
        third = exchange(parts)

        def arrive():
            second()
            third()

        return first, arrive

    for d, where, narrow in ((LEFT, pl.ds(0, 8), pl.ds(0, 4)), (RIGHT, pl.ds(16, 8), pl.ds(12, 4))):
        @pl.when(jnp.logical_not(can[d]))
        def _(where=where, narrow=narrow):
            for buffer in ext:
                buffer[:, where, 8:40, :] = jnp.zeros((4, 8, 32, 128), F32)
            coef[:, narrow, 8:24, :] = jnp.zeros((4, 4, 16, 128), F32)
    for d, where, narrow in ((BELOW, pl.ds(8, 8), pl.ds(0, 8)), (ABOVE, pl.ds(32, 8), pl.ds(24, 8))):
        @pl.when(jnp.logical_not(can[d]))
        def _(where=where, narrow=narrow):
            for buffer in ext:
                buffer[:, 4:20, where, :] = jnp.zeros((4, 16, 8, 128), F32)
            coef[:, 4:12, narrow, :] = jnp.zeros((4, 8, 8, 128), F32)
    srecv[...] = jnp.zeros_like(srecv)
    precv[...] = jnp.zeros_like(precv)
    trecv[...] = jnp.zeros_like(trecv)

    barrier = pltpu.get_barrier_semaphore()
    greet = [(off, 0) for off in (-3, -2, -1, 1, 2, 3)] + [(x, z) for x in (-1, 0, 1) for z in (-1, 1)]
    for x, z in greet:
        pl.semaphore_signal(
            barrier, inc=1, device_id=(lax.rem(a + x + strips, strips), lax.rem(b + z + bands, bands)),
            device_id_type=MESH,
        )

    def put_stack(q, x):
        high, low = halves(jnp.concatenate([x, jnp.zeros((8, NT), F32)], axis=0))
        ds[q, 0:32, :] = high
        ds[q, 32:64, :] = low
        ds[q, 64:96, :] = high

    def rotate(left):
        for q in range(NQ):
            rot[q] = dot(left[...], ds[q])

    def contract(p0):
        total = None
        for q in range(NQ):
            for d in range(3):
                term = jac[pl.ds(p0, 3), q, d : d + 1, :] * rot[q, d * NBP : (d + 1) * NBP, :][None]
                total = term if total is None else total + term
        return total

    ksc[...] = jnp.zeros_like(ksc)
    tsc[...] = jnp.zeros_like(tsc)
    lsc[...] = jnp.zeros_like(lsc)
    smt[...] = jnp.zeros_like(smt)
    nmt[...] = jnp.zeros_like(nmt)
    integ[...] = jnp.zeros_like(integ)
    ds[:, 96:128, :] = jnp.zeros((NQ, 32, NT), BF16)
    local["stiff"].wait()
    for d in range(3):
        ksc[d * NBP : d * NBP + NB, 0:NB] = stiff_ref[d]
    kp[...] = (-stacked_left(ksc[0:80], 32)).astype(BF16)
    local["sol"].wait()
    for q in range(NQ):
        integ[q, 0:NB, :] = TIME_STEP * sol[q]
    for q in range(NQ):
        put_stack(q, integ[q] * (1.0 / TIME_STEP))
    local["jac"].wait()
    weight = TIME_STEP
    for degree in range(1, ORDERS):
        weight = weight * TIME_STEP / (degree + 1)
        rotate(kp)

        def step(i, carry, weight=weight, last=degree == ORDERS - 1):
            now = contract(3 * i)
            for k in range(3):
                total = integ[3 * i + k] + weight * now[k]
                integ[3 * i + k] = total
                put_stack(3 * i + k, total if last else now[k])
            return carry

        lax.fori_loop(0, 3, step, 0)

    local["trace"].wait()
    for f in range(4):
        rows = trace_ref[:, f, :]
        tsc[f * NJP : f * NJP + NJ, 0:NB] = rows
        tsc[f * NJP + NJ : f * NJP + NJ + 1, 0:NB] = jnp.sum(rows, axis=0, keepdims=True) * (1.0 / NJ)
    ts[...] = stacked_left(tsc[...], 32).astype(BF16)

    def names(start, count):
        these = iota((count, NT), 0) + start
        return [jnp.where(these == nbr_ref[f : f + 1, :], 1.0, 0.0).astype(BF16) for f in range(4)]

    local["nbr"].wait()
    for f, block in enumerate(names(1536, 128)):
        nmat[1536:1664, f * NT : (f + 1) * NT] = block
    local["surf"].wait()
    local["normal"].wait()
    for i in range(3):
        smt[i, 0:REACH, 0:CAP] = surf_ref[:, i, :].astype(F32)
        nmt[i, 0:REACH, 0:CAP] = normal_ref[:, i, :]
    own_cells = lane_row(smt[1])
    coupled = lane_row(smt[2])
    normals = [lane_row(nmt[c]) for c in range(3)]

    for q in reversed(range(NQ)):
        traces = dot(ts[...], ds[q])
        own[q] = traces
        high, low = halves(traces)
        for f in range(4):
            rows, cols = slice(f * NJP, (f + 1) * NJP), slice(f * NT, (f + 1) * NT)
            ohl[q * NJP : (q + 1) * NJP, cols] = high[rows]
            ohl[(NQ + q) * NJP : (NQ + q + 1) * NJP, cols] = low[rows]
    surf_names = nmat[1536:1664, :]
    at_faces = dot_nt(ohl[96:144, :], surf_names) + dot_nt(ohl[240:288, :], surf_names)
    speed = jnp.zeros((1, 128), F32)
    for c in range(3):
        speed = speed + normals[c] * at_faces[c * NJP + NJ : c * NJP + NJ + 1, :]
    own_speed = coupled * speed
    stile[...] = jnp.where(iota((8, 128), 0) == 0, own_speed, own_cells)

    pl.semaphore_wait(barrier, len(greet))
    speeds_arrive = surface(stile, lambda off: srecv.at[3 - off], 1, 3)
    pressure_first, first_arrive = send_first()

    local["lifting"].wait()
    for f in range(4):
        lsc[f * NJP : f * NJP + NJ, 0:NB] = lift_ref[:, f, :]
    flipped = jnp.transpose(ksc[...])[0:NBP]
    lanes = iota((NBP, 128), 1)
    turned = [jnp.where(lanes < NBP, flipped if d == 0 else pltpu.roll(flipped, 128 - d * NBP, 1), 0.0) for d in range(3)]
    turned.append(jnp.zeros((8, 128), F32))
    kv[...] = stacked_left(jnp.concatenate(turned, axis=0), 32).astype(BF16)
    lift = jnp.transpose(lsc[...])[0:32]
    lift_high = lift.astype(BF16).astype(F32)
    ls[:, 0:128] = (lift_high + pltpu.roll(lift_high, 64, 1)).astype(BF16)
    ls[:, 128:256] = (lift - lift_high).astype(BF16)
    shift = lax.rem(iota((256, 128), 0), 128) - iota((256, 128), 1)
    taps = jnp.zeros((256, 128), F32)
    for m, tap in enumerate(TAPS, 1):
        taps = jnp.where(shift == m, tap, jnp.where(shift == -m, -tap, taps))
    wy[...] = taps.astype(BF16)

    slot_row = iota((1, 128), 1) // CAP

    def combine(block, mine, buffer, row):
        total = jnp.zeros((1, 128), F32)
        for r in range(REACH):
            gap = block - (r - 2)
            if gap == 0:
                total = jnp.where(slot_row == r, mine, total)
            else:
                ok = (a + gap >= 0) & (a + gap < strips)
                total = jnp.where(slot_row == jnp.where(ok, r, -1), buffer[gap + 3, row : row + 1, :], total)
        return total

    pieces = (((8, 8), (8, 32), (4, 8), (0, 32)), ((4, 4), (16, 16), (0, 4), (8, 16)), ((16, 4), (16, 16), (12, 4), (8, 16)))
    middle = ((8, 8), (16, 16), (4, 8), (8, 16))

    def view(ref, f, box, dx=0, dz=0):
        (x, nx), (z, nz) = box[:2]
        return ref[f, x + dx : x + dx + nx, z + dz : z + dz + nz, :]

    def tap_sum(pick):
        total = None
        for m, tap in enumerate(TAPS, 1):
            term = tap * (pick(m) - pick(-m))
            total = term if total is None else total + term
        return total

    def along_x(ref, f, box):
        return tap_sum(lambda m: view(ref, f, box, dx=m))

    def along_z(ref, f, box):
        return tap_sum(lambda m: view(ref, f, box, dz=m))

    def along_y(ref, f, box):
        x = view(ref, f, box)
        shape = x.shape
        x = x.reshape(shape[0] * shape[1], 128)
        return dot(jnp.concatenate(halves(x), axis=1), wy[...]).reshape(shape)

    def coefs(f, box):
        (x, nx), (z, nz) = box[2:]
        return coef[f, x : x + nx, z : z + nz, :]

    def gradient(ref, f, box):
        return along_x(ref, f, box), along_z(ref, f, box), along_y(ref, f, box)

    def blown(slopes, box):
        return coefs(0, box) * slopes[0] + coefs(1, box) * slopes[1] + coefs(2, box) * slopes[2]

    def put(ref, box, value):
        (x, nx), (z, nz) = box[2:]
        ref[x : x + nx, z : z + nz, :] = value

    def get(ref, box):
        (x, nx), (z, nz) = box[2:]
        return ref[x : x + nx, z : z + nz, :]

    def squeeze(ref, box):
        return coefs(3, box) * (along_x(ref, 1, box) + along_z(ref, 2, box) + along_y(ref, 3, box))

    def names_block(i, carry):
        start = pl.multiple_of(64 * i, 64)
        for f, block in enumerate(names(start, 64)):
            nmat[pl.ds(start, 64), f * NT : (f + 1) * NT] = block
        return carry

    lax.fori_loop(0, 24, names_block, 0)
    given = dot_nt(ohl[...], nmat[1024:1664, :])
    given = given[0:144] + given[144:288]
    for d in range(4):
        for q in range(NQ):
            tout[d, q * NJ : (q + 1) * NJ, :] = given[q * NJP : q * NJP + NJ, d * RIM : (d + 1) * RIM]
    traces_arrive = exchange([(d, tout.at[d], trecv.at[mirror_of[d]]) for d in range(4)])
    own_at = given[:, 512:640]

    local["air"].wait()
    speeds_arrive()
    start_pressure[...] = e0[0, own_x, own_z, :].reshape(128, 128)
    for block in (-1, 0, 1):
        arrived = combine(block, own_speed, srecv, 0)
        cells = combine(block, own_cells, srecv, 1).astype(jnp.int32)
        cell_rows = lax.shift_right_logical(cells, 7)
        cell_lanes = lax.bitwise_and(cells, 127)
        at_row = jnp.where(iota((128, 128), 0) == cell_rows, arrived, 0.0)
        at_lane = jnp.where(iota((128, 128), 0) == cell_lanes, 1.0, 0.0).astype(BF16)
        if block == 0:
            own_rows = cell_rows
            bt[...] = at_lane
        gained[block + 1] = dot_nt(
            jnp.concatenate(halves(at_row), axis=1), jnp.concatenate([at_lane, at_lane], axis=1)
        ).reshape(8, 16, 128)
    e0[0, own_x, own_z, :] = e0[0, own_x, own_z, :] + gained[1]
    pressure_first()
    for block in (-1, 1):
        where = pl.ds(8 + 8 * block, 8)
        e0[0, where, own_z, :] = e0[0, where, own_z, :] + gained[block + 1]
    pressure_arrive = exchange(send_pressure_z(e0))

    picked = dot(jnp.concatenate(thirds(start_pressure[...]), axis=0), bt[...])
    picked = picked[0:128] + picked[128:256] + picked[256:384]
    looked = jnp.sum(jnp.where(iota((128, 128), 0) == own_rows, picked, 0.0), axis=0, keepdims=True)
    ptile[...] = jnp.broadcast_to(looked, (8, 128))
    replies_arrive = surface(ptile, lambda off: precv.at[off + 2], -1, 2)

    first_arrive()
    local["wind"].wait()
    local["bulk"].wait()
    local["lift"].wait()
    for box in pieces:
        (x, nx), (z, nz) = box[2:]
        coef[:, x : x + nx, z : z + nz, :] = coef[:, x : x + nx, z : z + nz, :] * TAP_UNIT
    lift_of[...] = lift_of[...] * TAP_UNIT
    for box in pieces:
        put(base, box, squeeze(e0, box))

    def shadow_first():
        for f in range(4):
            cols = slice(f * NT, (f + 1) * NT)
            gathered = dot(ohl[...], nmat[0:SLOTS, cols])
            gathered = gathered[0:144] + gathered[144:288]
            for q in range(NQ):
                rows = slice(f * NJP, (f + 1) * NJP)
                diff[q, rows, :] = gathered[q * NJP : (q + 1) * NJP] - own[q, rows, :]

    def shadow_second():
        rotate(kv)

        def step(i, carry):
            vol[pl.ds(3 * i, 3)] = contract(3 * i)
            return carry

        lax.fori_loop(0, 3, step, 0)

    def shadow_third():
        replies_arrive()
        traces_arrive()
        replies = jnp.where(slot_row == 2, looked, 0.0)
        for r in (0, 1, 3, 4):
            ok = (a + r - 2 >= 0) & (a + r - 2 < strips)
            replies = jnp.where(slot_row == jnp.where(ok, r, -1), precv[r, 0:1, :], replies)
        replies = coupled * replies
        row_q = iota((NQ * NJP, 128), 0) // NJP
        mirrored = jnp.where(row_q < 3, -2.0 * replies - own_at, own_at)
        for half, values in enumerate(halves(mirrored)):
            rl[half * 144 : half * 144 + 144, 512:640] = values
        for d in range(4):
            for q in range(NQ):
                x = jnp.concatenate([trecv[d, q * NJ : (q + 1) * NJ, :], jnp.zeros((NJP - NJ, RIM), F32)], axis=0)
                for half, values in enumerate(halves(x)):
                    start = half * 144 + q * NJP
                    rl[start : start + NJP, d * RIM : (d + 1) * RIM] = values
        for f in range(4):
            cols = slice(f * NT, (f + 1) * NT)
            gathered = dot(rl[...], nmat[SLOTS:1664, cols])
            gathered = gathered[0:144] + gathered[144:288]
            for q in range(NQ):
                rows = slice(f * NJP, (f + 1) * NJP)
                diff[q, rows, :] = diff[q, rows, :] + gathered[q * NJP : (q + 1) * NJP]

    def shadow_fourth():
        local["flx"].wait()

        def step(i, carry):
            faces = []
            for f in range(4):
                total = None
                for q in range(NQ):
                    term = flx[pl.ds(3 * i, 3), q, f : f + 1, :] * diff[q, f * NJP : (f + 1) * NJP, :][None]
                    total = term if total is None else total + term
                faces.append(total)
            fluxed = jnp.concatenate(faces, axis=1)
            for k in range(3):
                high, low = halves(fluxed[k])
                lifted = dot(ls[:, 0:192], jnp.concatenate([high, low, high], axis=0))
                p = 3 * i + k
                sout[p] = sol[p] + (vol[p] + lifted[0:NBP])[0:NB]
            return carry

        lax.fori_loop(0, 3, step, 0)

    for f in range(3):
        adv[f] = view(e0, 1 + f, middle) - blown(gradient(e0, 1 + f, middle), middle)
    shadow_first()
    for substep in range(SUBSTEPS):
        here = ext[substep]
        final = substep == SUBSTEPS - 1
        pressure_arrive()
        if substep == 0:
            for box in pieces:
                put(pe, box, view(here, 0, box) - get(base, box) - blown(gradient(here, 0, box), box))
        else:
            for box in pieces:
                put(base, box, view(here, 0, box) - blown(gradient(here, 0, box), box))
            velocity_arrive()
            for box in pieces:
                put(pe, box, get(base, box) - squeeze(here, box))
            for f in range(3):
                adv[f] = view(here, 1 + f, middle) - blown(gradient(here, 1 + f, middle), middle)
        if not final:
            there = ext[substep + 1]
            there[0, 4:20, own_z, :] = pe[:, 8:24, :]
            pressure_arrive = send_pressure(there)
        slopes = [tap_sum(lambda m: pe[4 + m : 12 + m, 8:24, :]), tap_sum(lambda m: pe[4:12, 8 + m : 24 + m, :])]
        x = pe[4:12, 8:24, :].reshape(128, 128)
        slopes.append(dot(jnp.concatenate(halves(x), axis=1), wy[...]).reshape(8, 16, 128))
        for f in range(3):
            value = adv[f] - lift_of[...] * slopes[f]
            if final:
                uout[1 + f] = value
            else:
                there[1 + f, own_x, own_z, :] = value
        if final:
            uout[0] = pe[4:12, 8:24, :]
        else:
            velocity_arrive = send_speeds(there)
            if substep == 0:
                shadow_second()
            else:
                shadow_third()
                shadow_fourth()

    fetch("sol_out", sout, sol_out)
    fetch("air_out", uout, air_out)
    local["sol_out"].wait()
    local["air_out"].wait()
    for ok, copy in pending:
        pl.when(ok)(copy.wait_send)


def vmem(*shape, dtype=F32):
    return pltpu.VMEM(shape, dtype)


def solution(mesh):
    strips, bands = mesh.shape["gx"], mesh.shape["gz"]

    def shards(
        solid_state, jacobians, flux_solvers, stiffness, trace_matrix, lift_matrix,
        neighbours, send_faces, surface_map, surface_normals, air_state, wind_field, air_medium,
    ):
        def body(*refs):
            kernel(strips, bands, *refs)

        hbm = pl.BlockSpec(memory_space=pl.ANY)
        return pl.pallas_call(
            body,
            out_shape=(
                jax.ShapeDtypeStruct(solid_state.shape, F32),
                jax.ShapeDtypeStruct(air_state.shape, F32),
            ),
            in_specs=[hbm] * 12,
            out_specs=(hbm, hbm),
            scratch_shapes=[
                vmem(3, NB, NB), vmem(NJ, 4, NB), vmem(NJ, 4, NB), vmem(4, NT, dtype=jnp.int32),
                vmem(REACH, 3, CAP, dtype=jnp.int32), vmem(REACH, 3, CAP),
                vmem(NQ, NB, NT), vmem(NQ, NQ, 3, NT), vmem(NQ, NQ, 4, NT),
                vmem(4, 24, 48, 128), vmem(4, 24, 48, 128), vmem(4, 24, 48, 128),
                vmem(4, 16, 32, 128), vmem(16, 32, 128), vmem(8, 16, 128),
                vmem(NQ, 128, NT, dtype=BF16), vmem(NQ, 80, NT), vmem(NQ, NBP, NT), vmem(NQ, 64, NT),
                vmem(288, SLOTS, dtype=BF16), vmem(1664, SLOTS, dtype=BF16), vmem(NQ, 64, NT),
                vmem(NQ, NBP, NT), vmem(NQ, NB, NT), vmem(4, 8, 16, 128),
                vmem(128, 128), vmem(128, 128), vmem(64, 128),
                vmem(80, 128, dtype=BF16), vmem(80, 128, dtype=BF16), vmem(64, 128, dtype=BF16),
                vmem(32, 256, dtype=BF16), vmem(256, 128, dtype=BF16),
                vmem(3, 8, 128), vmem(3, 8, 128),
                vmem(16, 32, 128), vmem(3, 8, 16, 128), vmem(128, 128), vmem(3, 8, 16, 128), vmem(128, 128, dtype=BF16),
                vmem(8, 128), vmem(8, 128),
                vmem(7, 8, 128), vmem(REACH, 8, 128),
                vmem(4, 96, RIM), vmem(4, 96, RIM), vmem(288, 640, dtype=BF16),
                pltpu.SemaphoreType.DMA((16,)),
                pltpu.SemaphoreType.DMA((96,)),
                pltpu.SemaphoreType.DMA((96,)),
            ],
            compiler_params=pltpu.CompilerParams(
                collective_id=0, has_side_effects=True, vmem_limit_bytes=56 * 1024 * 1024
            ),
            name="coupled_step",
        )(
            solid_state,
            jnp.transpose(jacobians, (1, 2, 0, 3)),
            jnp.transpose(flux_solvers, (1, 2, 0, 3)),
            stiffness,
            jnp.transpose(trace_matrix, (1, 0, 2)),
            jnp.transpose(lift_matrix, (2, 0, 1)),
            neighbours,
            jnp.transpose(surface_map, (1, 0, 2)),
            jnp.transpose(surface_normals, (1, 0, 2)),
            air_state, wind_field, air_medium,
        )

    in_specs = (
        P(None, None, ("gx", "gz")),
        P(None, None, None, ("gx", "gz")),
        P(None, None, None, ("gx", "gz")),
        P(),
        P(),
        P(),
        P(None, ("gx", "gz")),
        P(None, ("gx", "gz")),
        P(None, None, ("gx", "gz")),
        P(None, None, ("gx", "gz")),
        P(None, "gx", "gz", None),
        P(None, "gx", "gz", None),
        P(None, "gx", "gz", None),
    )
    out_specs = (P(None, None, ("gx", "gz")), P(None, "gx", "gz", None))
    return jax.shard_map(shards, mesh=mesh, in_specs=in_specs, out_specs=out_specs, check_vma=False)
```

time: 61.5 us -> 50 us (0.81)
  local copies, waits for them, and re-layouts: 8.52 us -> 2.38 us
  Pallas kernels: 52 us -> 46.5 us
    unnamed x18 -> x4, local copies, waits for them, and re-layouts: 8.52 us -> 2.38 us
    pallas_call x1, Pallas kernels: 52 us -> 46.5 us  [shards(): pl.pallas_call(body, out_shape=(jax.ShapeDtypeStruct(solid_state.shape, F...]
where the time goes in v1:
time: 50 us; the launch traced here: 49.5 us
  Pallas kernels  46.5 us (93%)
  local copies, waits for them, and re-layouts  2.38 us (5%)
  between operations  0.65 us (1%)
    pallas_call x1, Pallas kernels, shards(): pl.pallas_call(body, out_shape=(jax.ShapeDtypeStruct(solid_state.shape, F...  46.5 us
    unnamed x4, local copies, waits for them, and re-layouts  2.38 us

profile of v1, /device:TPU:25, one launch (start us, length us, event | category | flops | bytes accessed | tf_op | source)
XLA Modules:
  0.0 49.5 jit_solution(4349778555912376256)
XLA Ops:
  0.6 46.5 %coupled_step.1 = (f32[9,20,256]{2,1,0:T(8,128)}, f32[4,8,16,128]{3,2,1,0:T(8,128)}) custom-call(f32[9,20,256]{2,1,0:T(8,128)} %refs_0_.1, f32[9,9,3,256]{3,2,1,0:T(4,128)} %bitcast.6, f32[9,9,4,256]{3,2,1,0:T(4,128)} %bitcast.7, f32[3,20,20]{2,1,0:T(8,128)} %refs_3_.1, f32[10,4,20]{2,1,0:T(4,128)} %bitcast.8, f32[10,4,20]{2,1,0:T(4,128)} %bitcast.9, ...), custom_call_target="tpu_custom_call" | custom-call | tf_op jit(solution)/shard_map/coupled_step/pallas_call | solution.py:603
  47.1 0.0 copy-start
  47.1 1.7 %copy.16 = f32[9,20,256]{2,1,0:T(8,128)} copy(f32[9,20,256]{2,1,0:T(8,128)} %get-tuple-element.4) | data formatting | bytes 368640
  48.8 0.0 copy-done
  48.8 0.7 %copy.17 = f32[4,8,16,128]{3,2,1,0:T(8,128)} copy(f32[4,8,16,128]{3,2,1,0:T(8,128)S(1)} %copy-done) | data formatting | bytes 524288
Async XLA Ops:
  47.1 1.7 %copy-start = (f32[4,8,16,128]{3,2,1,0:T(8,128)S(1)}, f32[4,8,16,128]{3,2,1,0:T(8,128)}, u32[]{:S(2)}) copy-start(f32[4,8,16,128]{3,2,1,0:T(8,128)} %get-tuple-element.5) | copy-start | bytes 786436

commit v2 on v1

--- a/solution.py
+++ b/solution.py
@@ -69,7 +69,7 @@
         sol, jac, flx, e0, e1, e2, coef, pe, lift_of,
         ds, rot, integ, own, ohl, nmat, diff, vol, sout, uout,
         ksc, lsc, tsc, kp, kv, ts, ls, wy, smt, nmt,
-        base, adv, start_pressure, gained, bt,
+        base, adv, start_pressure, gained, bt, packed, corners,
         stile, ptile, srecv, precv, tout, trecv, rl,
         local_sem, send_sem, recv_sem,
     ) = refs
@@ -175,7 +175,30 @@
     coef_z = {BELOW: pl.ds(24, 8), ABOVE: pl.ds(0, 8)}
     with_arms = pl.ds(4, 16)
 
-    def send_speeds(buffer, raw=None):
+    corner_x = {LEFT: (8, 16), RIGHT: (12, 4)}
+    corner_z = {BELOW: (16, 32), ABOVE: (28, 12)}
+
+    def send_corners(buffer, turn):
+        parts = []
+        for i, d in enumerate(diagonals):
+            x, z = corner_x[d[0]][0], corner_z[d[1]][0]
+            for plane in range(4):
+                half = 4 * (plane % 2)
+                packed[turn, i, :, plane // 2, half : half + 4, :] = buffer[1:3, x + plane, z : z + 4, :]
+            parts.append((d, packed.at[turn, i], corners.at[turn, i]))
+        arrive = exchange(parts)
+
+        def unpack():
+            arrive()
+            for i, d in enumerate(diagonals):
+                x, z = corner_x[d[0]][1], corner_z[d[1]][1]
+                for plane in range(4):
+                    half = 4 * (plane % 2)
+                    buffer[1:3, x + plane, z : z + 4, :] = corners[turn, i, :, plane // 2, half : half + 4, :]
+
+        return unpack
+
+    def send_speeds(buffer, turn, raw=None):
         parts = []
         for d in (LEFT, RIGHT):
             if raw is None:
@@ -184,17 +207,19 @@
             else:
                 parts.append((d, raw.at[1], buffer.at[1, all_land[d], own_z]))
                 parts.append((d, raw.at[pl.ds(2, 2), raw_x[d]], buffer.at[pl.ds(2, 2), near_land[d], own_z]))
-        for d in diagonals:
-            src = buffer.at[pl.ds(1, 2), x_near[d[0]], z_near[d[1]]]
-            if raw is not None:
-                src = raw.at[pl.ds(1, 2), raw_x[d[0]], raw_z[d[1]]]
-            parts.append((d, src, buffer.at[pl.ds(1, 2), near_land[d[0]], z_land[d[1]]]))
         for d in (BELOW, ABOVE):
             src = buffer.at[pl.ds(1, 3), own_x, z_near[d]]
             if raw is not None:
                 src = raw.at[pl.ds(1, 3), :, raw_z[d]]
             parts.append((d, src, buffer.at[pl.ds(1, 3), own_x, z_land[d]]))
-        return exchange(parts)
+        sides = exchange(parts)
+        unpack = send_corners(buffer, turn)
+
+        def arrive():
+            sides()
+            unpack()
+
+        return arrive
 
     def send_pressure_z(buffer):
         return [(d, buffer.at[0, with_arms, z_near[d]], buffer.at[0, with_arms, z_land[d]]) for d in (BELOW, ABOVE)]
@@ -205,7 +230,8 @@
 
     def send_first():
         first = exchange([(d, air_h.at[0], e0.at[0, all_land[d], own_z]) for d in (LEFT, RIGHT)])
-        second = send_speeds(e0, air_h)
+        local["air"].wait()
+        second = send_speeds(e0, 0, air_h)
         parts = []
         for d in (LEFT, RIGHT):
             parts.append((d, wind_h.at[:, raw_x[d]], coef.at[pl.ds(0, 3), coef_x[d], coef_z_own]))
@@ -213,13 +239,14 @@
         for d in (BELOW, ABOVE):
             parts.append((d, wind_h.at[:, :, raw_z[d]], coef.at[pl.ds(0, 3), coef_x_own, coef_z[d]]))
             parts.append((d, med_h.at[0, :, raw_z[d]], coef.at[3, coef_x_own, coef_z[d]]))
-        third = exchange(parts)
+        third_parts = parts
 
         def arrive():
             second()
-            third()
-
-        return first, arrive
+            third[0]()
+
+        third = []
+        return first, arrive, lambda: third.append(exchange(third_parts))
 
     for d, where, narrow in ((LEFT, pl.ds(0, 8), pl.ds(0, 4)), (RIGHT, pl.ds(16, 8), pl.ds(12, 4))):
         @pl.when(jnp.logical_not(can[d]))
@@ -236,6 +263,7 @@
     srecv[...] = jnp.zeros_like(srecv)
     precv[...] = jnp.zeros_like(precv)
     trecv[...] = jnp.zeros_like(trecv)
+    corners[...] = jnp.zeros_like(corners)
 
     barrier = pltpu.get_barrier_semaphore()
     greet = [(off, 0) for off in (-3, -2, -1, 1, 2, 3)] + [(x, z) for x in (-1, 0, 1) for z in (-1, 1)]
@@ -245,21 +273,23 @@
             device_id_type=MESH,
         )
 
-    def put_stack(q, x):
-        high, low = halves(jnp.concatenate([x, jnp.zeros((8, NT), F32)], axis=0))
-        ds[q, 0:32, :] = high
-        ds[q, 32:64, :] = low
-        ds[q, 64:96, :] = high
+    lane_halves = (slice(0, 128), slice(128, 256))
+
+    def put_stack(cols, x):
+        high, low = halves(jnp.concatenate([x, jnp.zeros((NQ, 8, 128), F32)], axis=1))
+        ds[:, 0:32, cols] = high
+        ds[:, 32:64, cols] = low
+        ds[:, 64:96, cols] = high
 
     def rotate(left):
         for q in range(NQ):
             rot[q] = dot(left[...], ds[q])
 
-    def contract(p0):
+    def contract(cols):
         total = None
         for q in range(NQ):
             for d in range(3):
-                term = jac[pl.ds(p0, 3), q, d : d + 1, :] * rot[q, d * NBP : (d + 1) * NBP, :][None]
+                term = jac[:, q, d : d + 1, cols] * rot[q, d * NBP : (d + 1) * NBP, cols][None]
                 total = term if total is None else total + term
         return total
 
@@ -277,23 +307,22 @@
     local["sol"].wait()
     for q in range(NQ):
         integ[q, 0:NB, :] = TIME_STEP * sol[q]
-    for q in range(NQ):
-        put_stack(q, integ[q] * (1.0 / TIME_STEP))
+    for cols in lane_halves:
+        put_stack(cols, integ[:, :, cols] * (1.0 / TIME_STEP))
     local["jac"].wait()
     weight = TIME_STEP
     for degree in range(1, ORDERS):
         weight = weight * TIME_STEP / (degree + 1)
         rotate(kp)
-
-        def step(i, carry, weight=weight, last=degree == ORDERS - 1):
-            now = contract(3 * i)
-            for k in range(3):
-                total = integ[3 * i + k] + weight * now[k]
-                integ[3 * i + k] = total
-                put_stack(3 * i + k, total if last else now[k])
-            return carry
-
-        lax.fori_loop(0, 3, step, 0)
+        if degree==2:
+            pl.semaphore_wait(barrier, len(greet))
+            pressure_first, first_arrive, send_coefs = send_first()
+
+        for cols in lane_halves:
+            now = contract(cols)
+            total = integ[:, :, cols] + weight * now
+            integ[:, :, cols] = total
+            put_stack(cols, total if degree == ORDERS - 1 else now)
 
     local["trace"].wait()
     for f in range(4):
@@ -334,10 +363,9 @@
     own_speed = coupled * speed
     stile[...] = jnp.where(iota((8, 128), 0) == 0, own_speed, own_cells)
 
-    pl.semaphore_wait(barrier, len(greet))
     speeds_arrive = surface(stile, lambda off: srecv.at[3 - off], 1, 3)
-    pressure_first, first_arrive = send_first()
-
+
+    send_coefs()
     local["lifting"].wait()
     for f in range(4):
         lsc[f * NJP : f * NJP + NJ, 0:NB] = lift_ref[:, f, :]
@@ -431,7 +459,6 @@
     traces_arrive = exchange([(d, tout.at[d], trecv.at[mirror_of[d]]) for d in range(4)])
     own_at = given[:, 512:640]
 
-    local["air"].wait()
     speeds_arrive()
     start_pressure[...] = e0[0, own_x, own_z, :].reshape(128, 128)
     for block in (-1, 0, 1):
@@ -483,11 +510,8 @@
     def shadow_second():
         rotate(kv)
 
-        def step(i, carry):
-            vol[pl.ds(3 * i, 3)] = contract(3 * i)
-            return carry
-
-        lax.fori_loop(0, 3, step, 0)
+        for cols in lane_halves:
+            vol[:, :, cols] = contract(cols)
 
     def shadow_third():
         replies_arrive()
@@ -570,7 +594,7 @@
         if final:
             uout[0] = pe[4:12, 8:24, :]
         else:
-            velocity_arrive = send_speeds(there)
+            velocity_arrive = send_speeds(there, substep + 1)
             if substep == 0:
                 shadow_second()
             else:
@@ -600,7 +624,7 @@
             kernel(strips, bands, *refs)
 
         hbm = pl.BlockSpec(memory_space=pl.ANY)
-        return pl.pallas_call(
+        out = pl.pallas_call(
             body,
             out_shape=(
                 jax.ShapeDtypeStruct(solid_state.shape, F32),
@@ -622,6 +646,7 @@
                 vmem(32, 256, dtype=BF16), vmem(256, 128, dtype=BF16),
                 vmem(3, 8, 128), vmem(3, 8, 128),
                 vmem(16, 32, 128), vmem(3, 8, 16, 128), vmem(128, 128), vmem(3, 8, 16, 128), vmem(128, 128, dtype=BF16),
+                vmem(3, 4, 2, 2, 8, 128), vmem(3, 4, 2, 2, 8, 128),
                 vmem(8, 128), vmem(8, 128),
                 vmem(7, 8, 128), vmem(REACH, 8, 128),
                 vmem(4, 96, RIM), vmem(4, 96, RIM), vmem(288, 640, dtype=BF16),
@@ -645,6 +670,27 @@
             jnp.transpose(surface_normals, (1, 0, 2)),
             air_state, wind_field, air_medium,
         )
+        def hand(x, y, xo, yo, xv, yv, sem):
+            pairs = [(x, xv, xo)] + [(y.at[k], yv.at[k], yo.at[k]) for k in range(4)]
+            reads = [pltpu.make_async_copy(p[0], p[1], sem.at[0, i]) for i, p in enumerate(pairs)]
+            writes = [pltpu.make_async_copy(p[1], p[2], sem.at[1, i]) for i, p in enumerate(pairs)]
+            for r in reads:
+                r.start()
+            for r, w in zip(reads, writes):
+                r.wait()
+                w.start()
+            for w in writes:
+                w.wait()
+
+        return pl.pallas_call(
+            hand,
+            out_shape=(jax.ShapeDtypeStruct(solid_state.shape, F32), jax.ShapeDtypeStruct(air_state.shape, F32)),
+            in_specs=[hbm, hbm],
+            out_specs=(hbm, hbm),
+            scratch_shapes=[vmem(*solid_state.shape), vmem(*air_state.shape), pltpu.SemaphoreType.DMA((2, 5))],
+            compiler_params=pltpu.CompilerParams(vmem_limit_bytes=60 * 1024 * 1024),
+            name="hand_over",
+        )(*out)
 
     in_specs = (
         P(None, None, ("gx", "gz")),

time: 50 us -> 45.1 us (0.902)
  local copies, waits for them, and re-layouts: 2.38 us -> 0 us
  Pallas kernels: 46.5 us -> 44.4 us
    pallas_call x1, Pallas kernels: 46.5 us -> 42.6 us  [shards(): pl.pallas_call(body, out_shape=(jax.ShapeDtypeStruct(solid_state.shape, F...]
    unnamed x4 -> x0, local copies, waits for them, and re-layouts: 2.38 us -> none
    pallas_call x0 -> x1, Pallas kernels: none -> 1.79 us  [shards(): pl.pallas_call(hand, out_shape=(jax.ShapeDtypeStruct(solid_state.shape, F...]
where the time goes in v2:
time: 45.1 us; the launch traced here: 45 us
  Pallas kernels  44.4 us (98%)
  between operations  0.64 us (1%)
    pallas_call x1, Pallas kernels, shards(): pl.pallas_call(body, out_shape=(jax.ShapeDtypeStruct(solid_state.shape, F...  42.6 us
    pallas_call x1, Pallas kernels, shards(): pl.pallas_call(hand, out_shape=(jax.ShapeDtypeStruct(solid_state.shape, F...  1.79 us

profile of v2, /device:TPU:25, one launch (start us, length us, event | category | flops | bytes accessed | tf_op | source)
XLA Modules:
  0.0 45.0 jit_solution(12437001817105300888)
XLA Ops:
  0.6 42.6 %coupled_step.1 = (f32[9,20,256]{2,1,0:T(8,128)}, f32[4,8,16,128]{3,2,1,0:T(8,128)}) custom-call(f32[9,20,256]{2,1,0:T(8,128)} %refs_0_.1, f32[9,9,3,256]{3,2,1,0:T(4,128)} %bitcast.6, f32[9,9,4,256]{3,2,1,0:T(4,128)} %bitcast.7, f32[3,20,20]{2,1,0:T(8,128)} %refs_3_.1, f32[10,4,20]{2,1,0:T(4,128)} %bitcast.8, f32[10,4,20]{2,1,0:T(4,128)} %bitcast.9, ...), custom_call_target="tpu_custom_call" | custom-call | tf_op jit(solution)/shard_map/coupled_step/pallas_call | solution.py:627
  43.2 1.8 %hand_over.1 = (f32[9,20,256]{2,1,0:T(8,128)}, f32[4,8,16,128]{3,2,1,0:T(8,128)}) custom-call(f32[9,20,256]{2,1,0:T(8,128)} %get-tuple-element.4.x, f32[4,8,16,128]{3,2,1,0:T(8,128)} %get-tuple-element.5.y), custom_call_target="tpu_custom_call" | custom-call | tf_op jit(solution)/shard_map/hand_over/pallas_call | solution.py:685

commit v3 on v2

--- a/solution.py
+++ b/solution.py
@@ -69,7 +69,7 @@
         sol, jac, flx, e0, e1, e2, coef, pe, lift_of,
         ds, rot, integ, own, ohl, nmat, diff, vol, sout, uout,
         ksc, lsc, tsc, kp, kv, ts, ls, wy, smt, nmt,
-        base, adv, start_pressure, gained, bt, packed, corners,
+        base, adv, start_pressure, gained, bt, packed, corners, beyond, added,
         stile, ptile, srecv, precv, tout, trecv, rl,
         local_sem, send_sem, recv_sem,
     ) = refs
@@ -117,20 +117,31 @@
         )
 
     def exchange(parts):
-        copies = []
+        groups = {}
         for d, src, dst in parts:
-            ok, device = side(d)
-            copy = remote(src, dst, device, sem_count[0])
+            groups.setdefault(d, []).append(remote(src, dst, side(d)[1], sem_count[0]))
             sem_count[0] += 1
-            pl.when(ok)(copy.start)
-            pending.append((ok, copy))
-            copies.append((d, copy))
+        for d, copies in groups.items():
+            pl.when(side(d)[0])(every(copies, "start"))
+            pending.append((side(d)[0], copies))
 
         def arrive():
-            for d, copy in copies:
-                pl.when(side(opposite(d))[0])(copy.wait_recv)
+            for d, copies in groups.items():
+                pl.when(side(opposite(d))[0])(every(copies, "wait_recv"))
 
         return arrive
+
+    def every(copies, name):
+        def act():
+            for copy in copies:
+                getattr(copy, name)()
+
+        return act
+
+    def settle():
+        for ok, copies in pending:
+            pl.when(ok)(every(copies, "wait_send"))
+        pending.clear()
 
     def opposite(d):
         return tuple(mirror_of[k] for k in d) if isinstance(d, tuple) else mirror_of[d]
@@ -152,7 +163,7 @@
             copy = remote(src, place(off), (jnp.clip(to, 0, strips - 1), b), sem_count[0])
             sem_count[0] += 1
             pl.when(to_ok)(copy.start)
-            pending.append((to_ok, copy))
+            pending.append((to_ok, [copy]))
             waits.append((from_ok, copy))
 
         def arrive():
@@ -163,10 +174,7 @@
 
     diagonals = ((LEFT, BELOW), (LEFT, ABOVE), (RIGHT, BELOW), (RIGHT, ABOVE))
     x_near = {LEFT: pl.ds(8, 4), RIGHT: pl.ds(12, 4)}
-    x_far = {LEFT: pl.ds(12, 4), RIGHT: pl.ds(8, 4)}
     near_land = {LEFT: pl.ds(16, 4), RIGHT: pl.ds(4, 4)}
-    far_land = {LEFT: pl.ds(20, 4), RIGHT: pl.ds(0, 4)}
-    all_land = {LEFT: pl.ds(16, 8), RIGHT: pl.ds(0, 8)}
     z_near = {BELOW: pl.ds(16, 8), ABOVE: pl.ds(24, 8)}
     z_land = {BELOW: pl.ds(32, 8), ABOVE: pl.ds(8, 8)}
     raw_x = {LEFT: pl.ds(0, 4), RIGHT: pl.ds(4, 4)}
@@ -198,20 +206,11 @@
 
         return unpack
 
-    def send_speeds(buffer, turn, raw=None):
-        parts = []
-        for d in (LEFT, RIGHT):
-            if raw is None:
-                parts.append((d, buffer.at[1, own_x, own_z], buffer.at[1, all_land[d], own_z]))
-                parts.append((d, buffer.at[pl.ds(2, 2), x_near[d], own_z], buffer.at[pl.ds(2, 2), near_land[d], own_z]))
-            else:
-                parts.append((d, raw.at[1], buffer.at[1, all_land[d], own_z]))
-                parts.append((d, raw.at[pl.ds(2, 2), raw_x[d]], buffer.at[pl.ds(2, 2), near_land[d], own_z]))
+    def send_speeds(buffer, turn):
+        some = pl.ds(1, 3)
+        parts = [(d, buffer.at[some, x_near[d], own_z], buffer.at[some, near_land[d], own_z]) for d in (LEFT, RIGHT)]
         for d in (BELOW, ABOVE):
-            src = buffer.at[pl.ds(1, 3), own_x, z_near[d]]
-            if raw is not None:
-                src = raw.at[pl.ds(1, 3), :, raw_z[d]]
-            parts.append((d, src, buffer.at[pl.ds(1, 3), own_x, z_land[d]]))
+            parts.append((d, buffer.at[pl.ds(1, 3), own_x, z_near[d]], buffer.at[pl.ds(1, 3), own_x, z_land[d]]))
         sides = exchange(parts)
         unpack = send_corners(buffer, turn)
 
@@ -221,17 +220,36 @@
 
         return arrive
 
+    def send_beyond(buffer, turn, unit=1.0):
+        for d in (LEFT, RIGHT):
+            for plane in range(4):
+                x = 8 + plane if d == LEFT else 12 + plane
+                parts = []
+                for f in (0, 1):
+                    total = None
+                    for m, tap in enumerate(TAPS, 1):
+                        other = x + m if d == LEFT else x - m
+                        if (d == LEFT) == (other >= 12):
+                            term = tap * buffer[f, other, 16:32, :]
+                            total = term if total is None else total + term
+                    parts.append(total)
+                value = unit * (coef[0, x - 4, 8:24, :] * parts[0] + coef[3, x - 4, 8:24, :] * parts[1])
+                beyond[turn, d, plane] = -value if d == LEFT else value
+        return exchange([(d, beyond.at[turn, d], added.at[turn, mirror_of[d]]) for d in (LEFT, RIGHT)])
+
     def send_pressure_z(buffer):
         return [(d, buffer.at[0, with_arms, z_near[d]], buffer.at[0, with_arms, z_land[d]]) for d in (BELOW, ABOVE)]
 
     def send_pressure(buffer):
-        parts = [(d, buffer.at[0, x_far[d], own_z], buffer.at[0, far_land[d], own_z]) for d in (LEFT, RIGHT)]
-        return exchange(parts + send_pressure_z(buffer))
+        return exchange(send_pressure_z(buffer))
 
     def send_first():
-        first = exchange([(d, air_h.at[0], e0.at[0, all_land[d], own_z]) for d in (LEFT, RIGHT)])
         local["air"].wait()
-        second = send_speeds(e0, 0, air_h)
+        local["wind"].wait()
+        local["bulk"].wait()
+        first = exchange([(d, air_h.at[0, raw_x[d]], e0.at[0, near_land[d], own_z]) for d in (LEFT, RIGHT)])
+        second = send_beyond(e0, 0, TAP_UNIT)
+        fourth = send_speeds(e0, 0)
         parts = []
         for d in (LEFT, RIGHT):
             parts.append((d, wind_h.at[:, raw_x[d]], coef.at[pl.ds(0, 3), coef_x[d], coef_z_own]))
@@ -243,6 +261,7 @@
 
         def arrive():
             second()
+            fourth()
             third[0]()
 
         third = []
@@ -264,6 +283,10 @@
     precv[...] = jnp.zeros_like(precv)
     trecv[...] = jnp.zeros_like(trecv)
     corners[...] = jnp.zeros_like(corners)
+    added[...] = jnp.zeros_like(added)
+    for buffer in ext:
+        for x in (0, 20):
+            buffer[0:2, x : x + 4, 16:32, :] = jnp.zeros((2, 4, 16, 128), F32)
 
     barrier = pltpu.get_barrier_semaphore()
     greet = [(off, 0) for off in (-3, -2, -1, 1, 2, 3)] + [(x, z) for x in (-1, 0, 1) for z in (-1, 1)]
@@ -304,6 +327,29 @@
     for d in range(3):
         ksc[d * NBP : d * NBP + NB, 0:NB] = stiff_ref[d]
     kp[...] = (-stacked_left(ksc[0:80], 32)).astype(BF16)
+    local["trace"].wait()
+    for f in range(4):
+        rows = trace_ref[:, f, :]
+        tsc[f * NJP : f * NJP + NJ, 0:NB] = rows
+        tsc[f * NJP + NJ : f * NJP + NJ + 1, 0:NB] = jnp.sum(rows, axis=0, keepdims=True) * (1.0 / NJ)
+    ts[...] = stacked_left(tsc[...], 32).astype(BF16)
+
+    def names(start, count):
+        these = iota((count, NT), 0) + start
+        return [jnp.where(these == nbr_ref[f : f + 1, :], 1.0, 0.0).astype(BF16) for f in range(4)]
+
+    local["nbr"].wait()
+    for f, block in enumerate(names(1536, 128)):
+        nmat[1536:1664, f * NT : (f + 1) * NT] = block
+    local["surf"].wait()
+    local["normal"].wait()
+    for i in range(3):
+        smt[i, 0:REACH, 0:CAP] = surf_ref[:, i, :].astype(F32)
+        nmt[i, 0:REACH, 0:CAP] = normal_ref[:, i, :]
+    own_cells = lane_row(smt[1])
+    coupled = lane_row(smt[2])
+    normals = [lane_row(nmt[c]) for c in range(3)]
+
     local["sol"].wait()
     for q in range(NQ):
         integ[q, 0:NB, :] = TIME_STEP * sol[q]
@@ -324,30 +370,7 @@
             integ[:, :, cols] = total
             put_stack(cols, total if degree == ORDERS - 1 else now)
 
-    local["trace"].wait()
-    for f in range(4):
-        rows = trace_ref[:, f, :]
-        tsc[f * NJP : f * NJP + NJ, 0:NB] = rows
-        tsc[f * NJP + NJ : f * NJP + NJ + 1, 0:NB] = jnp.sum(rows, axis=0, keepdims=True) * (1.0 / NJ)
-    ts[...] = stacked_left(tsc[...], 32).astype(BF16)
-
-    def names(start, count):
-        these = iota((count, NT), 0) + start
-        return [jnp.where(these == nbr_ref[f : f + 1, :], 1.0, 0.0).astype(BF16) for f in range(4)]
-
-    local["nbr"].wait()
-    for f, block in enumerate(names(1536, 128)):
-        nmat[1536:1664, f * NT : (f + 1) * NT] = block
-    local["surf"].wait()
-    local["normal"].wait()
-    for i in range(3):
-        smt[i, 0:REACH, 0:CAP] = surf_ref[:, i, :].astype(F32)
-        nmt[i, 0:REACH, 0:CAP] = normal_ref[:, i, :]
-    own_cells = lane_row(smt[1])
-    coupled = lane_row(smt[2])
-    normals = [lane_row(nmt[c]) for c in range(3)]
-
-    for q in reversed(range(NQ)):
+    def put_traces(q):
         traces = dot(ts[...], ds[q])
         own[q] = traces
         high, low = halves(traces)
@@ -355,6 +378,9 @@
             rows, cols = slice(f * NJP, (f + 1) * NJP), slice(f * NT, (f + 1) * NT)
             ohl[q * NJP : (q + 1) * NJP, cols] = high[rows]
             ohl[(NQ + q) * NJP : (NQ + q + 1) * NJP, cols] = low[rows]
+
+    for q in (6, 7, 8):
+        put_traces(q)
     surf_names = nmat[1536:1664, :]
     at_faces = dot_nt(ohl[96:144, :], surf_names) + dot_nt(ohl[240:288, :], surf_names)
     speed = jnp.zeros((1, 128), F32)
@@ -366,6 +392,9 @@
     speeds_arrive = surface(stile, lambda off: srecv.at[3 - off], 1, 3)
 
     send_coefs()
+    for q in range(6):
+        put_traces(q)
+
     local["lifting"].wait()
     for f in range(4):
         lsc[f * NJP : f * NJP + NJ, 0:NB] = lift_ref[:, f, :]
@@ -488,15 +517,14 @@
     replies_arrive = surface(ptile, lambda off: precv.at[off + 2], -1, 2)
 
     first_arrive()
-    local["wind"].wait()
-    local["bulk"].wait()
     local["lift"].wait()
     for box in pieces:
         (x, nx), (z, nz) = box[2:]
         coef[:, x : x + nx, z : z + nz, :] = coef[:, x : x + nx, z : z + nz, :] * TAP_UNIT
     lift_of[...] = lift_of[...] * TAP_UNIT
-    for box in pieces:
-        put(base, box, squeeze(e0, box))
+    for box, d in zip(pieces, (None, LEFT, RIGHT)):
+        value = squeeze(e0, box)
+        put(base, box, value if d is None else value - added[0, d])
 
     def shadow_first():
         for f in range(4):
@@ -573,40 +601,46 @@
         else:
             for box in pieces:
                 put(base, box, view(here, 0, box) - blown(gradient(here, 0, box), box))
-            velocity_arrive()
-            for box in pieces:
-                put(pe, box, get(base, box) - squeeze(here, box))
+            beyond_arrive()
+            rest_arrive()
+            for box, d in zip(pieces, (None, LEFT, RIGHT)):
+                value = get(base, box) - squeeze(here, box)
+                put(pe, box, value if d is None else value + added[substep, d])
             for f in range(3):
                 adv[f] = view(here, 1 + f, middle) - blown(gradient(here, 1 + f, middle), middle)
         if not final:
             there = ext[substep + 1]
             there[0, 4:20, own_z, :] = pe[:, 8:24, :]
             pressure_arrive = send_pressure(there)
-        slopes = [tap_sum(lambda m: pe[4 + m : 12 + m, 8:24, :]), tap_sum(lambda m: pe[4:12, 8 + m : 24 + m, :])]
-        x = pe[4:12, 8:24, :].reshape(128, 128)
-        slopes.append(dot(jnp.concatenate(halves(x), axis=1), wy[...]).reshape(8, 16, 128))
-        for f in range(3):
-            value = adv[f] - lift_of[...] * slopes[f]
+        def take(f, slope):
+            value = adv[f] - lift_of[...] * slope
             if final:
                 uout[1 + f] = value
             else:
                 there[1 + f, own_x, own_z, :] = value
+
+        take(0, tap_sum(lambda m: pe[4 + m : 12 + m, 8:24, :]))
+        if not final:
+            beyond_arrive = send_beyond(there, substep + 1)
+        take(1, tap_sum(lambda m: pe[4:12, 8 + m : 24 + m, :]))
+        x = pe[4:12, 8:24, :].reshape(128, 128)
+        take(2, dot(jnp.concatenate(halves(x), axis=1), wy[...]).reshape(8, 16, 128))
         if final:
             uout[0] = pe[4:12, 8:24, :]
         else:
-            velocity_arrive = send_speeds(there, substep + 1)
+            rest_arrive = send_speeds(there, substep + 1)
             if substep == 0:
                 shadow_second()
             else:
                 shadow_third()
                 shadow_fourth()
+                settle()
 
     fetch("sol_out", sout, sol_out)
     fetch("air_out", uout, air_out)
     local["sol_out"].wait()
     local["air_out"].wait()
-    for ok, copy in pending:
-        pl.when(ok)(copy.wait_send)
+    settle()
 
 
 def vmem(*shape, dtype=F32):
@@ -647,6 +681,7 @@
                 vmem(3, 8, 128), vmem(3, 8, 128),
                 vmem(16, 32, 128), vmem(3, 8, 16, 128), vmem(128, 128), vmem(3, 8, 16, 128), vmem(128, 128, dtype=BF16),
                 vmem(3, 4, 2, 2, 8, 128), vmem(3, 4, 2, 2, 8, 128),
+                vmem(3, 2, 4, 16, 128), vmem(3, 2, 4, 16, 128),
                 vmem(8, 128), vmem(8, 128),
                 vmem(7, 8, 128), vmem(REACH, 8, 128),
                 vmem(4, 96, RIM), vmem(4, 96, RIM), vmem(288, 640, dtype=BF16),

time: 45.1 us -> 43.1 us (0.956)
  Pallas kernels: 44.4 us -> 42.4 us
    pallas_call x1, Pallas kernels: 42.6 us -> 40.6 us  [shards(): pl.pallas_call(body, out_shape=(jax.ShapeDtypeStruct(solid_state.shape, F...]
where the time goes in v3:
time: 43.1 us; the launch traced here: 43 us
  Pallas kernels  42.4 us (98%)
  between operations  0.64 us (1%)
    pallas_call x1, Pallas kernels, shards(): pl.pallas_call(body, out_shape=(jax.ShapeDtypeStruct(solid_state.shape, F...  40.6 us
    pallas_call x1, Pallas kernels, shards(): pl.pallas_call(hand, out_shape=(jax.ShapeDtypeStruct(solid_state.shape, F...  1.79 us

profile of v3, /device:TPU:25, one launch (start us, length us, event | category | flops | bytes accessed | tf_op | source)
XLA Modules:
  0.0 43.0 jit_solution(11967776204975145427)
XLA Ops:
  0.6 40.6 %coupled_step.1 = (f32[9,20,256]{2,1,0:T(8,128)}, f32[4,8,16,128]{3,2,1,0:T(8,128)}) custom-call(f32[9,20,256]{2,1,0:T(8,128)} %refs_0_.1, f32[9,9,3,256]{3,2,1,0:T(4,128)} %bitcast.6, f32[9,9,4,256]{3,2,1,0:T(4,128)} %bitcast.7, f32[3,20,20]{2,1,0:T(8,128)} %refs_3_.1, f32[10,4,20]{2,1,0:T(4,128)} %bitcast.8, f32[10,4,20]{2,1,0:T(4,128)} %bitcast.9, ...), custom_call_target="tpu_custom_call" | custom-call | tf_op jit(solution)/shard_map/coupled_step/pallas_call | solution.py:661
  41.2 1.8 %hand_over.1 = (f32[9,20,256]{2,1,0:T(8,128)}, f32[4,8,16,128]{3,2,1,0:T(8,128)}) custom-call(f32[9,20,256]{2,1,0:T(8,128)} %get-tuple-element.4.x, f32[4,8,16,128]{3,2,1,0:T(8,128)} %get-tuple-element.5.y), custom_call_target="tpu_custom_call" | custom-call | tf_op jit(solution)/shard_map/hand_over/pallas_call | solution.py:720

commit v4 on v3

--- a/solution.py
+++ b/solution.py
@@ -209,16 +209,17 @@
     def send_speeds(buffer, turn):
         some = pl.ds(1, 3)
         parts = [(d, buffer.at[some, x_near[d], own_z], buffer.at[some, near_land[d], own_z]) for d in (LEFT, RIGHT)]
-        for d in (BELOW, ABOVE):
-            parts.append((d, buffer.at[pl.ds(1, 3), own_x, z_near[d]], buffer.at[pl.ds(1, 3), own_x, z_land[d]]))
-        sides = exchange(parts)
+        strips_arrive = exchange(parts)
+        bands_arrive = exchange(
+            [(d, buffer.at[some, own_x, z_near[d]], buffer.at[some, own_x, z_land[d]]) for d in (BELOW, ABOVE)]
+        )
         unpack = send_corners(buffer, turn)
 
         def arrive():
-            sides()
+            strips_arrive()
             unpack()
 
-        return arrive
+        return bands_arrive, arrive
 
     def send_beyond(buffer, turn, unit=1.0):
         for d in (LEFT, RIGHT):
@@ -249,7 +250,7 @@
         local["bulk"].wait()
         first = exchange([(d, air_h.at[0, raw_x[d]], e0.at[0, near_land[d], own_z]) for d in (LEFT, RIGHT)])
         second = send_beyond(e0, 0, TAP_UNIT)
-        fourth = send_speeds(e0, 0)
+        fourth, fifth = send_speeds(e0, 0)
         parts = []
         for d in (LEFT, RIGHT):
             parts.append((d, wind_h.at[:, raw_x[d]], coef.at[pl.ds(0, 3), coef_x[d], coef_z_own]))
@@ -262,6 +263,7 @@
         def arrive():
             second()
             fourth()
+            fifth()
             third[0]()
 
         third = []
@@ -360,7 +362,7 @@
     for degree in range(1, ORDERS):
         weight = weight * TIME_STEP / (degree + 1)
         rotate(kp)
-        if degree==2:
+        if degree == 1:
             pl.semaphore_wait(barrier, len(greet))
             pressure_first, first_arrive, send_coefs = send_first()
 
@@ -601,21 +603,32 @@
         else:
             for box in pieces:
                 put(base, box, view(here, 0, box) - blown(gradient(here, 0, box), box))
+            bands_arrive()
+            center, left, right = pieces
+            put(base, center, get(base, center) - coefs(3, center) * (along_z(here, 2, center) + along_y(here, 3, center)))
+            for f in range(3):
+                adv[f] = view(here, 1 + f, middle) - (
+                    coefs(1, middle) * along_z(here, 1 + f, middle) + coefs(2, middle) * along_y(here, 1 + f, middle)
+                )
             beyond_arrive()
-            rest_arrive()
-            for box, d in zip(pieces, (None, LEFT, RIGHT)):
-                value = get(base, box) - squeeze(here, box)
-                put(pe, box, value if d is None else value + added[substep, d])
+            strips_arrive()
+            put(pe, center, get(base, center) - coefs(3, center) * along_x(here, 1, center))
+            for box, d in ((left, LEFT), (right, RIGHT)):
+                put(pe, box, get(base, box) - squeeze(here, box) + added[substep, d])
             for f in range(3):
-                adv[f] = view(here, 1 + f, middle) - blown(gradient(here, 1 + f, middle), middle)
+                adv[f] = adv[f] - coefs(0, middle) * along_x(here, 1 + f, middle)
         if not final:
             there = ext[substep + 1]
             there[0, 4:20, own_z, :] = pe[:, 8:24, :]
             pressure_arrive = send_pressure(there)
+        else:
+            uout[0] = pe[4:12, 8:24, :]
+            fetch("air_out0", uout.at[0], air_out.at[0])
         def take(f, slope):
             value = adv[f] - lift_of[...] * slope
             if final:
                 uout[1 + f] = value
+                fetch(f"air_out{1 + f}", uout.at[1 + f], air_out.at[1 + f])
             else:
                 there[1 + f, own_x, own_z, :] = value
 
@@ -625,21 +638,19 @@
         take(1, tap_sum(lambda m: pe[4:12, 8 + m : 24 + m, :]))
         x = pe[4:12, 8:24, :].reshape(128, 128)
         take(2, dot(jnp.concatenate(halves(x), axis=1), wy[...]).reshape(8, 16, 128))
-        if final:
-            uout[0] = pe[4:12, 8:24, :]
-        else:
-            rest_arrive = send_speeds(there, substep + 1)
+        if not final:
+            bands_arrive, strips_arrive = send_speeds(there, substep + 1)
             if substep == 0:
                 shadow_second()
             else:
                 shadow_third()
                 shadow_fourth()
+                fetch("sol_out", sout, sol_out)
                 settle()
 
-    fetch("sol_out", sout, sol_out)
-    fetch("air_out", uout, air_out)
     local["sol_out"].wait()
-    local["air_out"].wait()
+    for f in range(4):
+        local[f"air_out{f}"].wait()
     settle()
 
 
@@ -685,7 +696,7 @@
                 vmem(8, 128), vmem(8, 128),
                 vmem(7, 8, 128), vmem(REACH, 8, 128),
                 vmem(4, 96, RIM), vmem(4, 96, RIM), vmem(288, 640, dtype=BF16),
-                pltpu.SemaphoreType.DMA((16,)),
+                pltpu.SemaphoreType.DMA((20,)),
                 pltpu.SemaphoreType.DMA((96,)),
                 pltpu.SemaphoreType.DMA((96,)),
             ],
@@ -706,7 +717,8 @@
             air_state, wind_field, air_medium,
         )
         def hand(x, y, xo, yo, xv, yv, sem):
-            pairs = [(x, xv, xo)] + [(y.at[k], yv.at[k], yo.at[k]) for k in range(4)]
+            thirds_of = [pl.ds(3 * k, 3) for k in range(3)]
+            pairs = [(x.at[k], xv.at[k], xo.at[k]) for k in thirds_of] + [(y.at[k], yv.at[k], yo.at[k]) for k in range(4)]
             reads = [pltpu.make_async_copy(p[0], p[1], sem.at[0, i]) for i, p in enumerate(pairs)]
             writes = [pltpu.make_async_copy(p[1], p[2], sem.at[1, i]) for i, p in enumerate(pairs)]
             for r in reads:
@@ -722,7 +734,7 @@
             out_shape=(jax.ShapeDtypeStruct(solid_state.shape, F32), jax.ShapeDtypeStruct(air_state.shape, F32)),
             in_specs=[hbm, hbm],
             out_specs=(hbm, hbm),
-            scratch_shapes=[vmem(*solid_state.shape), vmem(*air_state.shape), pltpu.SemaphoreType.DMA((2, 5))],
+            scratch_shapes=[vmem(*solid_state.shape), vmem(*air_state.shape), pltpu.SemaphoreType.DMA((2, 7))],
             compiler_params=pltpu.CompilerParams(vmem_limit_bytes=60 * 1024 * 1024),
             name="hand_over",
         )(*out)

time: 43.1 us -> 42.7 us (level)
  Pallas kernels: 42.4 us -> 41.9 us
    pallas_call x1, Pallas kernels: 40.6 us -> 40.1 us  [shards(): pl.pallas_call(body, out_shape=(jax.ShapeDtypeStruct(solid_state.shape, F...]
where the time goes in v4:
time: 42.7 us; the launch traced here: 42.5 us
  Pallas kernels  41.9 us (98%)
  between operations  0.64 us (1%)
    pallas_call x1, Pallas kernels, shards(): pl.pallas_call(body, out_shape=(jax.ShapeDtypeStruct(solid_state.shape, F...  40.1 us
    pallas_call x1, Pallas kernels, shards(): pl.pallas_call(hand, out_shape=(jax.ShapeDtypeStruct(solid_state.shape, F...  1.8 us

profile of v4, /device:TPU:25, one launch (start us, length us, event | category | flops | bytes accessed | tf_op | source)
XLA Modules:
  0.0 42.5 jit_solution(17457156319487599414)
XLA Ops:
  0.6 40.1 %coupled_step.1 = (f32[9,20,256]{2,1,0:T(8,128)}, f32[4,8,16,128]{3,2,1,0:T(8,128)}) custom-call(f32[9,20,256]{2,1,0:T(8,128)} %refs_0_.1, f32[9,9,3,256]{3,2,1,0:T(4,128)} %bitcast.6, f32[9,9,4,256]{3,2,1,0:T(4,128)} %bitcast.7, f32[3,20,20]{2,1,0:T(8,128)} %refs_3_.1, f32[10,4,20]{2,1,0:T(4,128)} %bitcast.8, f32[10,4,20]{2,1,0:T(4,128)} %bitcast.9, ...), custom_call_target="tpu_custom_call" | custom-call | tf_op jit(solution)/shard_map/coupled_step/pallas_call | solution.py:672
  40.7 1.8 %hand_over.1 = (f32[9,20,256]{2,1,0:T(8,128)}, f32[4,8,16,128]{3,2,1,0:T(8,128)}) custom-call(f32[9,20,256]{2,1,0:T(8,128)} %get-tuple-element.4.x, f32[4,8,16,128]{3,2,1,0:T(8,128)} %get-tuple-element.5.y), custom_call_target="tpu_custom_call" | custom-call | tf_op jit(solution)/shard_map/hand_over/pallas_call | solution.py:732

commit v5 on v4

--- a/solution.py
+++ b/solution.py
@@ -361,10 +361,10 @@
     weight = TIME_STEP
     for degree in range(1, ORDERS):
         weight = weight * TIME_STEP / (degree + 1)
-        rotate(kp)
         if degree == 1:
             pl.semaphore_wait(barrier, len(greet))
             pressure_first, first_arrive, send_coefs = send_first()
+        rotate(kp)
 
         for cols in lane_halves:
             now = contract(cols)

time: 42.7 us -> 42.7 us (level)
  no operation moved by 1% of the time
where the time goes in v5:
time: 42.7 us; the launch traced here: 42.5 us
  Pallas kernels  41.9 us (98%)
  between operations  0.64 us (1%)
    pallas_call x1, Pallas kernels, shards(): pl.pallas_call(body, out_shape=(jax.ShapeDtypeStruct(solid_state.shape, F...  40.1 us
    pallas_call x1, Pallas kernels, shards(): pl.pallas_call(hand, out_shape=(jax.ShapeDtypeStruct(solid_state.shape, F...  1.8 us

profile of v5, /device:TPU:25, one launch (start us, length us, event | category | flops | bytes accessed | tf_op | source)
XLA Modules:
  0.0 42.5 jit_solution(9518505726222800718)
XLA Ops:
  0.6 40.1 %coupled_step.1 = (f32[9,20,256]{2,1,0:T(8,128)}, f32[4,8,16,128]{3,2,1,0:T(8,128)}) custom-call(f32[9,20,256]{2,1,0:T(8,128)} %refs_0_.1, f32[9,9,3,256]{3,2,1,0:T(4,128)} %bitcast.6, f32[9,9,4,256]{3,2,1,0:T(4,128)} %bitcast.7, f32[3,20,20]{2,1,0:T(8,128)} %refs_3_.1, f32[10,4,20]{2,1,0:T(4,128)} %bitcast.8, f32[10,4,20]{2,1,0:T(4,128)} %bitcast.9, ...), custom_call_target="tpu_custom_call" | custom-call | tf_op jit(solution)/shard_map/coupled_step/pallas_call | solution.py:672
  40.7 1.8 %hand_over.1 = (f32[9,20,256]{2,1,0:T(8,128)}, f32[4,8,16,128]{3,2,1,0:T(8,128)}) custom-call(f32[9,20,256]{2,1,0:T(8,128)} %get-tuple-element.4.x, f32[4,8,16,128]{3,2,1,0:T(8,128)} %get-tuple-element.5.y), custom_call_target="tpu_custom_call" | custom-call | tf_op jit(solution)/shard_map/hand_over/pallas_call | solution.py:732
